TPU v7x, 512 devices: a whole 4x8x8 slice. The times are simulated.
512 devices in a mesh: dp: 64 (over y, x, core), mp: 8 (over z).
Axes of the slice: x: 4, y: 8, z: 8, core: 2. Of those that a mesh axis runs over, the one named last changes fastest.
Arguments:
- hidden_acts: bfloat16 [49152, 5120], P('dp', 'mp'), may hold values from -36 to 36, as said below
- out_grads: bfloat16 [49152, 2048], P('dp', 'mp'), may hold values from -0.25 to 0.25
- prev_factor: float32 [4, 2048], replicated, may hold values from -6 to 6
Outputs:
- basis: float32 [4, 5120], P(None, 'mp')
- factor: float32 [4, 2048], replicated
- residual: bfloat16 [64, 5120, 2048], P('dp', 'mp')
Inputs may be any that keep to these rules, and one draw needn't show every extreme that they name: `hidden_acts`: activations of hidden units, of varying scale from unit to unit.
All inputs are finite; a program needn't handle non-finite values.
Results may differ from a plain program's by a relative error of at most 0.00105.
Values may be sent and summed in bfloat16 or wider, within the bound.
No kernel may reach another device: no remote copies, remote signals or barrier semaphores. Data moves between devices by JAX's collectives and lax.ppermute only.
A program may use at most 64 MiB of HBM per device.

v0:
```python
import math

import jax
import jax.numpy as jnp
from jax import lax
from jax.sharding import PartitionSpec as P


def local(hidden_acts, out_grads, prev_factor):
    replicas = lax.axis_size("dp")
    tensor_ways = lax.axis_size("mp")
    highest = lax.Precision.HIGHEST
    grad_block = lax.dot_general(
        hidden_acts,
        lax.all_gather(out_grads, "mp", axis=1, tiled=True),
        (((0,), (0,)), ((), ())),
        preferred_element_type=jnp.float32,
    )
    basis_part = lax.dot_general(
        prev_factor,
        grad_block,
        (((1,), (1,)), ((), ())),
        precision=highest,
        preferred_element_type=jnp.float32,
    )
    raw = lax.psum(basis_part, "dp") / replicas
    rows = []
    for k in range(raw.shape[0]):
        vector = raw[k]
        if rows:
            stack = jnp.stack(rows)
            weights = lax.psum(jnp.dot(stack, vector, precision=highest), "mp")
            vector = vector - jnp.dot(weights, stack, precision=highest)
        length_sq = lax.psum(jnp.sum(vector * vector), "mp")
        rows.append(vector * lax.rsqrt(length_sq + 1e-06))
    unit_rows = jnp.stack(rows)
    partial_factor = jnp.dot(unit_rows, grad_block, precision=highest)
    factor = lax.psum(partial_factor, ("dp", "mp")) / replicas
    approx = jnp.dot(unit_rows.T, factor, precision=highest)
    residual = (grad_block - approx).astype(jnp.bfloat16)[None]
    full_units = hidden_acts.shape[1] * tensor_ways
    return (unit_rows * math.sqrt(full_units), factor, residual)


def solution(mesh):
    return jax.shard_map(
        local,
        mesh=mesh,
        in_specs=(P("dp", "mp"), P("dp", "mp"), P()),
        out_specs=(P(None, "mp"), P(), P("dp", "mp", None)),
        check_vma=False,
    )
```

profile of v0, /device:TPU:1, one launch (start us, length us, event | category | flops | bytes accessed | tf_op | source)
XLA Modules:
  0.0 564.1 jit_solution(9847485930219735607)
XLA Ops:
  7.2 0.0 copy-start
  7.2 0.0 copy-start.3
  7.2 0.0 all-gather.2.cloned.1.call-start
  7.2 0.7 all-gather.2.cloned.1.call-update
  7.9 63.4 %all-gather.2.cloned.1.call-done = bf16[768,2048]{1,0:T(8,128)(2,1)} async-done(((bf16[768,256]{1,0:T(8,128)(2,1)}), bf16[768,2048]{1,0:T(8,128)(2,1)}) %all-gather.2.cloned.1.call-update) | async-done | bytes 3145744 | tf_op jit(solution)/shard_map/all_gather | solution.py:15
  71.3 0.0 copy-done
  71.3 4.2 fusion.13
  75.5 0.0 copy-start.1
  75.5 2.3 copy-done.1
  77.8 0.0 copy-done.3
  77.8 4.5 convolution_bitcast_fusion
  82.2 245.1 %psum.63 = f32[4,640]{1,0:T(4,128)S(1)} all-reduce(f32[4,640]{1,0:T(4,128)S(1)} %convolution_bitcast_fusion), channel_id=1, replica_groups=mesh['dp'=64,'mp'=8] {'dp'}, use_global_device_ids=true, to_apply=%region_0.0 | all-reduce | flops 2560 | bytes 20480 | tf_op jit(solution)/shard_map/psum | solution.py:26
  327.4 0.6 multiply_reduce_fusion.4
  328.0 14.4 %psum.64 = f32[]{:T(128)} all-reduce(f32[]{:T(128)} %get-tuple-element.3), channel_id=1, replica_groups=mesh['dp'=64,'mp'=8] {'mp'}, use_global_device_ids=true, to_apply=%region_2.0 | all-reduce | flops 1 | bytes 8 | tf_op jit(solution)/shard_map/psum | solution.py:34
  343.1 0.6 multiply_reduce_fusion
  343.7 11.5 %psum.65 = f32[]{:T(128)} all-reduce(f32[]{:T(128)} %multiply_reduce_fusion), channel_id=1, replica_groups=mesh['dp'=64,'mp'=8] {'mp'}, use_global_device_ids=true, to_apply=%region_3.0 | all-reduce | flops 1 | bytes 8 | tf_op jit(solution)/shard_map/psum | solution.py:32
  355.2 1.2 multiply_reduce_fusion.3
  356.5 12.5 %psum.66 = f32[]{:T(128)} all-reduce(f32[]{:T(128)} %multiply_reduce_fusion.3), channel_id=1, replica_groups=mesh['dp'=64,'mp'=8] {'mp'}, use_global_device_ids=true, to_apply=%region_5.0 | all-reduce | flops 1 | bytes 8 | tf_op jit(solution)/shard_map/psum | solution.py:34
  369.7 0.7 broadcast_multiply_fusion.5
  370.4 0.1 convolution_bitcast_fusion.1
  370.5 10.9 %psum.67 = f32[2]{0:T(128)S(1)} all-reduce(f32[2]{0:T(128)S(1)} %convolution_bitcast_fusion.1), channel_id=1, replica_groups=mesh['dp'=64,'mp'=8] {'mp'}, use_global_device_ids=true, to_apply=%region_6.0 | all-reduce | flops 2 | bytes 16 | tf_op jit(solution)/shard_map/psum | solution.py:32
  381.4 0.2 convolution_reduce_fusion.1
  381.6 0.6 multiply_reduce_fusion.2
  382.2 13.1 %psum.68 = f32[]{:T(128)} all-reduce(f32[]{:T(128)} %get-tuple-element.9), channel_id=1, replica_groups=mesh['dp'=64,'mp'=8] {'mp'}, use_global_device_ids=true, to_apply=%region_8.0 | all-reduce | flops 1 | bytes 8 | tf_op jit(solution)/shard_map/psum | solution.py:34
  396.0 0.2 convolution_bitcast_fusion.2
  396.2 10.7 %psum.69 = f32[3]{0:T(128)S(1)} all-reduce(f32[3]{0:T(128)S(1)} %convolution_bitcast_fusion.2), channel_id=1, replica_groups=mesh['dp'=64,'mp'=8] {'mp'}, use_global_device_ids=true, to_apply=%region_9.0 | all-reduce | flops 3 | bytes 24 | tf_op jit(solution)/shard_map/psum | solution.py:32
  406.9 0.2 convolution_reduce_fusion
  407.1 0.6 multiply_reduce_fusion.1
  407.7 12.8 %psum.70 = f32[]{:T(128)} all-reduce(f32[]{:T(128)} %get-tuple-element.7), channel_id=1, replica_groups=mesh['dp'=64,'mp'=8] {'mp'}, use_global_device_ids=true, to_apply=%region_11.0 | all-reduce | flops 1 | bytes 8 | tf_op jit(solution)/shard_map/psum | solution.py:34
  421.1 0.6 broadcast_multiply_fusion.1
  421.7 5.1 fusion.11
  426.8 123.1 %psum.71 = f32[4,2048]{1,0:T(4,128)S(1)} all-reduce(f32[4,2048]{1,0:T(4,128)S(1)} %fusion.11), channel_id=1, replica_groups=mesh['dp'=64,'mp'=8] {'dp','mp'}, use_global_device_ids=true, to_apply=%region_12.0 | all-reduce | flops 8192 | bytes 65536 | tf_op jit(solution)/shard_map/psum | solution.py:38
  549.9 0.0 copy-start.2
  549.9 7.4 %fusion = bf16[1,640,2048]{2,1,0:T(8,128)(2,1)} fusion(f32[640,2048]{1,0:T(8,128)} %copy-done.1, f32[4,2048]{1,0:T(4,128)S(1)} %broadcast_multiply_fusion, f32[1,640]{1,0:T(1,128)S(1)} %stack.29, f32[1,640]{1,0:T(1,128)S(1)} %stack.27, f32[1,640]{1,0:T(1,128)S(1)} %stack.12, f32[1,640]{1,0:T(1,128)S(1)} %get-tuple-element.12), kind=kOutput, calls=%fused_computation.1 | convolution fusion | flops 65543680 | bytes 7907328 | tf_op jit(solution)/shard_map/dot_general | solution.py:39
  557.3 0.0 copy-done.2
  (8 shorter events, 0.0 us)
Async XLA Ops:
  7.2 64.1 %copy-start = (bf16[768,640]{1,0:T(8,128)(2,1)S(1)}, bf16[768,640]{1,0:T(8,128)(2,1)}, u32[]{:S(2)}) copy-start(bf16[768,640]{1,0:T(8,128)(2,1)} %param.3) | copy-start | bytes 2949124
  7.2 70.6 %copy-start.3 = (f32[4,2048]{1,0:T(4,128)S(1)}, f32[4,2048]{1,0:T(4,128)}, u32[]{:S(2)}) copy-start(f32[4,2048]{1,0:T(4,128)} %param.5) | copy-start | bytes 98308
  7.2 64.1 %all-gather.2.cloned.1.call-start = ((), (), s32[]{:S(2)}) async-start(), calls=%async_computation | async-start | bytes 3538944 | tf_op jit(solution)/shard_map/all_gather | solution.py:15
  75.5 2.3 copy-start.1
  549.9 7.4 %copy-start.2 = (f32[4,2048]{1,0:T(4,128)}, f32[4,2048]{1,0:T(4,128)S(1)}, u32[]{:S(2)}) copy-start(f32[4,2048]{1,0:T(4,128)S(1)} %broadcast_multiply_fusion) | copy-start | bytes 98308
Sparse Core Ops, SparseCore 0:
  10.0 61.2 all-gather.1
where the time goes:
time: 565 us; the launch traced here: 564 us
  blocking collectives  454 us (80%)
  waiting for transfers between devices  64 us (11%)
  matrix products  21.7 us (4%)
  between operations  16.9 us (3%)
    psum x1, blocking collectives, local(): raw = lax.psum(basis_part, 'dp') / replicas  245 us
    psum x1, blocking collectives, local(): factor = lax.psum(partial_factor, ('dp', 'mp')) / replicas  123 us
    all_gather x1, waiting for transfers between devices, local(): lax.all_gather(out_grads, 'mp', axis=1, tiled=True)  63.4 us
    psum x4, blocking collectives, local(): length_sq = lax.psum(jnp.sum(vector * vector), 'mp')  52.8 us
    psum x3, blocking collectives, local(): weights = lax.psum(jnp.dot(stack, vector, precision=highest), 'mp')  33.1 us
  transfers between devices with their start and end apart: 1, of which 1 were waited for; matrix products, arithmetic and copies ran while one was open for 0% of the time, Pallas kernels for 0%

commit v1 on v0

v1 whole, which is shorter than its diff:
```python
import functools
import math

import jax
import jax.numpy as jnp
from jax import lax
from jax.experimental import pallas as pl
from jax.experimental.pallas import tpu as pltpu
from jax.sharding import PartitionSpec as P

F32 = jnp.float32
BF16 = jnp.bfloat16
VMEM_BYTES = 40 * 1024 * 1024
PIECE_PAIRS = ((0, 0), (0, 1), (1, 0), (0, 2), (1, 1), (2, 0))


def pieces(x):
    high = x.astype(BF16).astype(F32)
    rest = x - high
    middle = rest.astype(BF16).astype(F32)
    low = (rest - middle).astype(BF16).astype(F32)
    return high, middle, low


def tree_sum(values):
    values = list(values)
    while len(values) > 1:
        values = [values[i] + values[i + 1] for i in range(0, len(values), 2)]
    return values[0]


def fold(product, rank):
    return product[:rank] + (product[rank:2 * rank] + product[2 * rank:3 * rank])


def stack_pieces(x, stack):
    rank = x.shape[0]
    stack[...] = jnp.zeros_like(stack)
    for i, piece in enumerate(pieces(x)):
        stack[rank * i:rank * (i + 1), :] = piece
    return stack[...].astype(BF16)


def coeff_kernel(prev_ref, grads_ref, out_ref, stack):
    width = grads_ref.shape[1]
    start = pl.multiple_of(lax.axis_index("mp") * width, width)
    rows = stack_pieces(prev_ref[:, pl.ds(start, width)], stack)
    product = lax.dot_general(
        rows, grads_ref[...], (((1,), (1,)), ((), ())), preferred_element_type=F32
    )
    out_ref[...] = fold(product, prev_ref.shape[0])


def left_kernel(*refs):
    *parts, acts_ref, out_ref, stack = refs
    rows = stack_pieces(tree_sum([p[...] for p in parts]), stack)
    product = jnp.dot(rows, acts_ref[...], preferred_element_type=F32)
    out_ref[...] = fold(product, out_ref.shape[0])


def back_kernel(scale, *refs):
    *parts, acts_ref, out_ref, stack = refs
    units = acts_ref.shape[1]
    raw = tree_sum([p[...] for p in parts]) * scale
    rows = stack_pieces(raw, stack)
    product = lax.dot_general(
        rows, acts_ref[...], (((1,), (1,)), ((), ())), preferred_element_type=F32
    )
    out_ref[:, :units] = raw
    out_ref[:, units:] = fold(product, out_ref.shape[0])


def right_kernel(units, *refs):
    *parts, grads_ref, out_ref, stack = refs
    rows = stack_pieces(tree_sum([p[:, units:] for p in parts]), stack)
    product = jnp.dot(rows, grads_ref[...], preferred_element_type=F32)
    out_ref[...] = fold(product, out_ref.shape[0])


def total(x):
    return jnp.sum(jnp.sum(x, axis=1, keepdims=True), axis=0, keepdims=True)


def basis_kernel(units, full_units, *refs):
    *parts, basis_ref, wide_ref, map_ref, rows, unit = refs
    rank = basis_ref.shape[0]
    me = lax.axis_index("mp")
    for k, part in enumerate(parts):
        place = jnp.bitwise_xor(me, k)
        for r in range(rank):
            rows[r, pl.ds(place, 1), :] = part[r:r + 1, :units]
    units_done, maps = [], []
    for k in range(rank):
        raw = rows[k]
        vector = raw
        line = [jnp.full((1, 1), 1.0 if j == k else 0.0, F32) for j in range(rank)]
        if k:
            weights = [total(u * raw) for u in units_done]
            vector = raw - functools.reduce(
                jnp.add, [w * u for w, u in zip(weights, units_done)]
            )
            for w, earlier in zip(weights, maps):
                line = [a - w * b for a, b in zip(line, earlier)]
        square = total(vector * vector) + 1e-06
        inverse = lax.rsqrt(square)
        inverse = inverse * (1.5 - 0.5 * (square * inverse) * inverse)
        units_done.append(vector * inverse)
        maps.append([a * inverse for a in line])
        unit[k] = units_done[k]
        for j in range(rank):
            map_ref[rank * k + j:rank * k + j + 1, :] = jnp.broadcast_to(maps[k][j], (1, 128))
    wide_ref[...] = jnp.zeros_like(wide_ref)
    for k in range(rank):
        mine = unit[k, pl.ds(me, 1), :]
        basis_ref[k:k + 1, :] = mine * math.sqrt(full_units)
        split = pieces(mine)
        for i, (a, _) in enumerate(PIECE_PAIRS):
            wide_ref[rank * i + k:rank * i + k + 1, :] = split[a]


def residual_kernel(scale, *refs):
    *parts, acts_ref, grads_ref, wide_ref, map_ref, factor_ref, out_ref, held = refs
    rank = factor_ref.shape[0]

    @pl.when(pl.program_id(0) == 0)
    def _():
        y = tree_sum([p[...] for p in parts]) * scale
        held[...] = jnp.zeros_like(held)
        for k in range(rank):
            line = functools.reduce(
                jnp.add,
                [map_ref[rank * k + j:rank * k + j + 1, 0:1] * y[j:j + 1] for j in range(rank)],
            )
            factor_ref[k:k + 1, :] = line
            split = pieces(line)
            for i, (_, b) in enumerate(PIECE_PAIRS):
                held[rank * i + k:rank * i + k + 1, :] = split[b]

    first = (((0,), (0,)), ((), ()))
    whole = lax.dot_general(acts_ref[...], grads_ref[...], first, preferred_element_type=F32)
    approx = lax.dot_general(
        wide_ref[...].astype(BF16), held[...].astype(BF16), first, preferred_element_type=F32
    )
    out_ref[0] = (whole - approx).astype(out_ref.dtype)


def call(kernel, outs, args, scratch, flops, grid=None):
    moved = sum(a.size * a.dtype.itemsize for a in args)
    moved += sum(o.size * o.dtype.itemsize for o in outs)
    single = len(outs) == 1
    return pl.pallas_call(
        kernel,
        out_shape=outs[0] if single else outs,
        scratch_shapes=scratch,
        compiler_params=pltpu.CompilerParams(vmem_limit_bytes=VMEM_BYTES),
        cost_estimate=pl.CostEstimate(flops=flops, bytes_accessed=moved, transcendentals=0),
        **(grid or {}),
    )(*args)


def exchange(x, axis, masks):
    size = lax.axis_size(axis)
    return [
        x if mask == 0 else lax.ppermute(x, axis, [(i, i ^ mask) for i in range(size)])
        for mask in masks
    ]


def local(hidden_acts, out_grads, prev_factor):
    tokens, units = hidden_acts.shape
    rank, width = prev_factor.shape
    replicas = lax.axis_size("dp")
    ways = lax.axis_size("mp")
    rows = lambda n: pltpu.VMEM((16, n), F32)
    shape = lambda *dims: jax.ShapeDtypeStruct(dims, F32)

    grads = lax.all_gather(out_grads, "mp", axis=1, tiled=True)

    coeffs = call(
        coeff_kernel, [shape(rank, tokens)], [prev_factor, out_grads],
        [rows(out_grads.shape[1])], 32 * tokens * out_grads.shape[1],
    )
    coeffs = exchange(coeffs, "mp", range(ways))
    left = call(
        left_kernel, [shape(rank, units)], [*coeffs, hidden_acts],
        [rows(tokens)], 32 * tokens * units,
    )
    for mask in (1, 2, 6, 8, 16):
        left = tree_sum(exchange(left, "dp", (0, mask)))
    packed = call(
        functools.partial(back_kernel, 1.0 / replicas), [shape(rank, units + tokens)],
        [*exchange(left, "dp", (0, 48)), hidden_acts],
        [rows(units)], 32 * tokens * units,
    )
    packed = exchange(packed, "mp", range(ways))
    right = call(
        functools.partial(right_kernel, units), [shape(rank, width)], [*packed, grads],
        [rows(tokens)], 32 * tokens * width,
    )
    basis, wide, maps = call(
        functools.partial(basis_kernel, units, units * ways),
        [shape(rank, units), shape(32, units), shape(rank * rank, 128)], packed,
        [pltpu.VMEM((rank, ways, units), F32), pltpu.VMEM((rank, ways, units), F32)],
        100 * ways * units,
    )
    right = tree_sum(exchange(right, "dp", (0, 1)))
    right = tree_sum(exchange(right, "dp", (0, 2, 4, 6)))
    right = exchange(right, "dp", range(0, 64, 8))

    tile = 128
    whole = lambda *dims: pl.BlockSpec(dims, lambda i: (0,) * len(dims))
    factor, residual = call(
        functools.partial(residual_kernel, 1.0 / replicas),
        [shape(rank, width), jax.ShapeDtypeStruct((1, units, width), BF16)],
        [*right, hidden_acts, grads, wide, maps],
        [pltpu.VMEM((32, width), F32)],
        2 * tokens * units * width,
        dict(
            grid=(units // tile,),
            in_specs=[whole(rank, width)] * len(right) + [
                pl.BlockSpec((tokens, tile), lambda i: (0, i)),
                whole(tokens, width),
                pl.BlockSpec((32, tile), lambda i: (0, i)),
                whole(rank * rank, 128),
            ],
            out_specs=[whole(rank, width), pl.BlockSpec((1, tile, width), lambda i: (0, i, 0))],
        ),
    )
    return basis, factor, residual


def solution(mesh):
    return jax.shard_map(
        local,
        mesh=mesh,
        in_specs=(P("dp", "mp"), P("dp", "mp"), P()),
        out_specs=(P(None, "mp"), P(), P("dp", "mp", None)),
        check_vma=False,
    )
```

time: 565 us -> 176 us (0.31)
  the two profiles are of different devices: /device:TPU:1 before, /device:TPU:4 now
where the time goes in v1:
time: 176 us; the launch traced here: 174 us
  starting transfers between devices  123 us (70%)
  waiting for transfers between devices  23.1 us (13%)
  between operations  14.4 us (8%)
  Pallas kernels  7.83 us (4%)
  local copies, waits for them, and re-layouts  6.06 us (3%)
    ppermute x31, starting transfers between devices, exchange(): lax.ppermute(x, axis, [(i, i ^ mask) for i in range(size)])  123 us
    ppermute x31, waiting for transfers between devices, exchange(): lax.ppermute(x, axis, [(i, i ^ mask) for i in range(size)])  22.4 us
    pallas_call x6, Pallas kernels, call(): pl.pallas_call(kernel, out_shape=outs[0] if single else outs, scratch_sha...  7.83 us
    unnamed x14, local copies, waits for them, and re-layouts  6.06 us
  transfers between devices with their start and end apart: 32, of which 11 were waited for; matrix products, arithmetic and copies ran while one was open for 0% of the time, Pallas kernels for 1%

profile of v1, /device:TPU:4, one launch (start us, length us, event | category | flops | bytes accessed | tf_op | source)
XLA Modules:
  0.0 174.5 jit_solution(3747434306636245953)
XLA Ops:
  7.9 1.0 copy-done.5
  9.9 11.0 %collective-permute-start.6 = (f32[4,768]{1,0:T(4,128)S(1)}, f32[4,768]{1,0:T(4,128)S(1)}, u32[]{:S(2)}, u32[]{:S(2)}) collective-permute-start(f32[4,768]{1,0:T(4,128)S(1)} %shard_map.58.refs_0_), channel_id=1, source_target_pairs={{0,7},{1,6},{2,5},{3,4},{4,3},{5,2},{6,1},{7,0},{8,15},{9,14},{10,... | collective-permute-start | bytes 36872 | tf_op jit(solution)/shard_map/ppermute | solution.py:164
  20.9 1.9 %collective-permute-start.5 = (f32[4,768]{1,0:T(4,128)S(1)}, f32[4,768]{1,0:T(4,128)S(1)}, u32[]{:S(2)}, u32[]{:S(2)}) collective-permute-start(f32[4,768]{1,0:T(4,128)S(1)} %shard_map.58.refs_0_), channel_id=1, source_target_pairs={{0,6},{1,7},{2,4},{3,5},{4,2},{5,3},{6,0},{7,1},{8,14},{9,15},{10,... | collective-permute-start | bytes 36872 | tf_op jit(solution)/shard_map/ppermute | solution.py:164
  22.8 5.1 %collective-permute-start.4 = (f32[4,768]{1,0:T(4,128)S(1)}, f32[4,768]{1,0:T(4,128)S(1)}, u32[]{:S(2)}, u32[]{:S(2)}) collective-permute-start(f32[4,768]{1,0:T(4,128)S(1)} %shard_map.58.refs_0_), channel_id=1, source_target_pairs={{0,5},{1,4},{2,7},{3,6},{4,1},{5,0},{6,3},{7,2},{8,13},{9,12},{10,... | collective-permute-start | bytes 36872 | tf_op jit(solution)/shard_map/ppermute | solution.py:164
  27.9 4.6 %collective-permute-start.3 = (f32[4,768]{1,0:T(4,128)S(1)}, f32[4,768]{1,0:T(4,128)S(1)}, u32[]{:S(2)}, u32[]{:S(2)}) collective-permute-start(f32[4,768]{1,0:T(4,128)S(1)} %shard_map.58.refs_0_), channel_id=1, source_target_pairs={{0,4},{1,5},{2,6},{3,7},{4,0},{5,1},{6,2},{7,3},{8,12},{9,13},{10,... | collective-permute-start | bytes 36872 | tf_op jit(solution)/shard_map/ppermute | solution.py:164
  32.6 3.4 %collective-permute-start.2 = (f32[4,768]{1,0:T(4,128)S(1)}, f32[4,768]{1,0:T(4,128)S(1)}, u32[]{:S(2)}, u32[]{:S(2)}) collective-permute-start(f32[4,768]{1,0:T(4,128)S(1)} %shard_map.58.refs_0_), channel_id=1, source_target_pairs={{0,3},{1,2},{2,1},{3,0},{4,7},{5,6},{6,5},{7,4},{8,11},{9,10},{10,... | collective-permute-start | bytes 36872 | tf_op jit(solution)/shard_map/ppermute | solution.py:164
  35.9 2.5 %collective-permute-start.1 = (f32[4,768]{1,0:T(4,128)S(1)}, f32[4,768]{1,0:T(4,128)S(1)}, u32[]{:S(2)}, u32[]{:S(2)}) collective-permute-start(f32[4,768]{1,0:T(4,128)S(1)} %shard_map.58.refs_0_), channel_id=1, source_target_pairs={{0,2},{1,3},{2,0},{3,1},{4,6},{5,7},{6,4},{7,5},{8,10},{9,11},{10,... | collective-permute-start | bytes 36872 | tf_op jit(solution)/shard_map/ppermute | solution.py:164
  38.4 4.3 %collective-permute-start = (f32[4,768]{1,0:T(4,128)S(1)}, f32[4,768]{1,0:T(4,128)S(1)}, u32[]{:S(2)}, u32[]{:S(2)}) collective-permute-start(f32[4,768]{1,0:T(4,128)S(1)} %shard_map.58.refs_0_), channel_id=1, source_target_pairs={{0,1},{1,0},{2,3},{3,2},{4,5},{5,4},{6,7},{7,6},{8,9},{9,8},{10,11... | collective-permute-start | bytes 36872 | tf_op jit(solution)/shard_map/ppermute | solution.py:164
  42.8 1.6 collective-permute-done.refs_1_
  44.4 1.2 copy-done
  45.8 2.1 %collective-permute-start.7 = (f32[4,640]{1,0:T(4,128)S(1)}, f32[4,640]{1,0:T(4,128)S(1)}, u32[]{:S(2)}, u32[]{:S(2)}) collective-permute-start(f32[4,640]{1,0:T(4,128)S(1)} %shard_map.59), channel_id=1, source_target_pairs={{0,8},{8,0},{16,24},{24,16},{32,40},{40,32},{48,56},{56,48},{64,72... | collective-permute-start | bytes 30728 | tf_op jit(solution)/shard_map/ppermute | solution.py:164
  47.9 1.1 collective-permute-done.7
  49.1 3.1 %collective-permute-start.8 = (f32[4,640]{1,0:T(4,128)S(1)}, f32[4,640]{1,0:T(4,128)S(1)}, u32[]{:S(2)}, u32[]{:S(2)}) collective-permute-start(f32[4,640]{1,0:T(4,128)S(1)} %add.27), channel_id=1, source_target_pairs={{0,16},{8,24},{16,0},{24,8},{32,48},{40,56},{48,32},{56,40},{64,80... | collective-permute-start | bytes 30728 | tf_op jit(solution)/shard_map/ppermute | solution.py:164
  52.2 2.5 %collective-permute-done.8 = f32[4,640]{1,0:T(4,128)S(1)} collective-permute-done((f32[4,640]{1,0:T(4,128)S(1)}, f32[4,640]{1,0:T(4,128)S(1)}, u32[]{:S(2)}, u32[]{:S(2)}) %collective-permute-start.8) | collective-permute-done | bytes 10272 | tf_op jit(solution)/shard_map/ppermute | solution.py:164
  54.6 2.4 %collective-permute-start.9 = (f32[4,640]{1,0:T(4,128)S(1)}, f32[4,640]{1,0:T(4,128)S(1)}, u32[]{:S(2)}, u32[]{:S(2)}) collective-permute-start(f32[4,640]{1,0:T(4,128)S(1)} %add.28), channel_id=1, source_target_pairs={{0,48},{8,56},{16,32},{24,40},{32,16},{40,24},{48,0},{56,8},{64,11... | collective-permute-start | bytes 30728 | tf_op jit(solution)/shard_map/ppermute | solution.py:164
  57.1 3.1 %collective-permute-done.9 = f32[4,640]{1,0:T(4,128)S(1)} collective-permute-done((f32[4,640]{1,0:T(4,128)S(1)}, f32[4,640]{1,0:T(4,128)S(1)}, u32[]{:S(2)}, u32[]{:S(2)}) %collective-permute-start.9) | collective-permute-done | bytes 10272 | tf_op jit(solution)/shard_map/ppermute | solution.py:164
  60.2 3.5 %collective-permute-start.10 = (f32[4,640]{1,0:T(4,128)S(1)}, f32[4,640]{1,0:T(4,128)S(1)}, u32[]{:S(2)}, u32[]{:S(2)}) collective-permute-start(f32[4,640]{1,0:T(4,128)S(1)} %add.29), channel_id=1, source_target_pairs={{0,64},{8,72},{16,80},{24,88},{32,96},{40,104},{48,112},{56,120},{... | collective-permute-start | bytes 30728 | tf_op jit(solution)/shard_map/ppermute | solution.py:164
  63.7 2.1 %collective-permute-done.10 = f32[4,640]{1,0:T(4,128)S(1)} collective-permute-done((f32[4,640]{1,0:T(4,128)S(1)}, f32[4,640]{1,0:T(4,128)S(1)}, u32[]{:S(2)}, u32[]{:S(2)}) %collective-permute-start.10) | collective-permute-done | bytes 10272 | tf_op jit(solution)/shard_map/ppermute | solution.py:164
  65.7 4.5 %collective-permute-start.11 = (f32[4,640]{1,0:T(4,128)S(1)}, f32[4,640]{1,0:T(4,128)S(1)}, u32[]{:S(2)}, u32[]{:S(2)}) collective-permute-start(f32[4,640]{1,0:T(4,128)S(1)} %add.30), channel_id=1, source_target_pairs={{0,128},{8,136},{16,144},{24,152},{32,160},{40,168},{48,176},{56,1... | collective-permute-start | bytes 30728 | tf_op jit(solution)/shard_map/ppermute | solution.py:164
  70.2 1.9 %collective-permute-done.11 = f32[4,640]{1,0:T(4,128)S(1)} collective-permute-done((f32[4,640]{1,0:T(4,128)S(1)}, f32[4,640]{1,0:T(4,128)S(1)}, u32[]{:S(2)}, u32[]{:S(2)}) %collective-permute-start.11) | collective-permute-done | bytes 10272 | tf_op jit(solution)/shard_map/ppermute | solution.py:164
  72.2 6.2 %collective-permute-start.12 = (f32[4,640]{1,0:T(4,128)S(1)}, f32[4,640]{1,0:T(4,128)S(1)}, u32[]{:S(2)}, u32[]{:S(2)}) collective-permute-start(f32[4,640]{1,0:T(4,128)S(1)} %add.31.refs_0_), channel_id=1, source_target_pairs={{0,384},{8,392},{16,400},{24,408},{32,416},{40,424},{48,432},{56,4... | collective-permute-start | bytes 30728 | tf_op jit(solution)/shard_map/ppermute | solution.py:164
  78.4 1.7 collective-permute-done.12.refs_1_
  80.1 1.2 copy-done.1
  81.7 5.7 %collective-permute-start.19 = (f32[4,1408]{1,0:T(4,128)S(1)}, f32[4,1408]{1,0:T(4,128)S(1)}, u32[]{:S(2)}, u32[]{:S(2)}) collective-permute-start(f32[4,1408]{1,0:T(4,128)S(1)} %shard_map.60.refs_0_), channel_id=1, source_target_pairs={{0,7},{1,6},{2,5},{3,4},{4,3},{5,2},{6,1},{7,0},{8,15},{9,14},{10,... | collective-permute-start | bytes 67592 | tf_op jit(solution)/shard_map/ppermute | solution.py:164
  87.4 3.7 %collective-permute-start.18 = (f32[4,1408]{1,0:T(4,128)S(1)}, f32[4,1408]{1,0:T(4,128)S(1)}, u32[]{:S(2)}, u32[]{:S(2)}) collective-permute-start(f32[4,1408]{1,0:T(4,128)S(1)} %shard_map.60.refs_0_), channel_id=1, source_target_pairs={{0,6},{1,7},{2,4},{3,5},{4,2},{5,3},{6,0},{7,1},{8,14},{9,15},{10,... | collective-permute-start | bytes 67592 | tf_op jit(solution)/shard_map/ppermute | solution.py:164
  91.1 4.2 %collective-permute-start.17 = (f32[4,1408]{1,0:T(4,128)S(1)}, f32[4,1408]{1,0:T(4,128)S(1)}, u32[]{:S(2)}, u32[]{:S(2)}) collective-permute-start(f32[4,1408]{1,0:T(4,128)S(1)} %shard_map.60.refs_0_), channel_id=1, source_target_pairs={{0,5},{1,4},{2,7},{3,6},{4,1},{5,0},{6,3},{7,2},{8,13},{9,12},{10,... | collective-permute-start | bytes 67592 | tf_op jit(solution)/shard_map/ppermute | solution.py:164
  95.3 4.7 %collective-permute-start.16 = (f32[4,1408]{1,0:T(4,128)S(1)}, f32[4,1408]{1,0:T(4,128)S(1)}, u32[]{:S(2)}, u32[]{:S(2)}) collective-permute-start(f32[4,1408]{1,0:T(4,128)S(1)} %shard_map.60.refs_0_), channel_id=1, source_target_pairs={{0,4},{1,5},{2,6},{3,7},{4,0},{5,1},{6,2},{7,3},{8,12},{9,13},{10,... | collective-permute-start | bytes 67592 | tf_op jit(solution)/shard_map/ppermute | solution.py:164
  100.0 3.4 %collective-permute-start.15 = (f32[4,1408]{1,0:T(4,128)S(1)}, f32[4,1408]{1,0:T(4,128)S(1)}, u32[]{:S(2)}, u32[]{:S(2)}) collective-permute-start(f32[4,1408]{1,0:T(4,128)S(1)} %shard_map.60.refs_0_), channel_id=1, source_target_pairs={{0,3},{1,2},{2,1},{3,0},{4,7},{5,6},{6,5},{7,4},{8,11},{9,10},{10,... | collective-permute-start | bytes 67592 | tf_op jit(solution)/shard_map/ppermute | solution.py:164
  103.4 3.3 %collective-permute-start.14 = (f32[4,1408]{1,0:T(4,128)S(1)}, f32[4,1408]{1,0:T(4,128)S(1)}, u32[]{:S(2)}, u32[]{:S(2)}) collective-permute-start(f32[4,1408]{1,0:T(4,128)S(1)} %shard_map.60.refs_0_), channel_id=1, source_target_pairs={{0,2},{1,3},{2,0},{3,1},{4,6},{5,7},{6,4},{7,5},{8,10},{9,11},{10,... | collective-permute-start | bytes 67592 | tf_op jit(solution)/shard_map/ppermute | solution.py:164
  106.7 3.4 %collective-permute-start.13 = (f32[4,1408]{1,0:T(4,128)S(1)}, f32[4,1408]{1,0:T(4,128)S(1)}, u32[]{:S(2)}, u32[]{:S(2)}) collective-permute-start(f32[4,1408]{1,0:T(4,128)S(1)} %shard_map.60.refs_0_), channel_id=1, source_target_pairs={{0,1},{1,0},{2,3},{3,2},{4,5},{5,4},{6,7},{7,6},{8,9},{9,8},{10,11... | collective-permute-start | bytes 67592 | tf_op jit(solution)/shard_map/ppermute | solution.py:164
  110.2 2.2 %collective-permute-done.13.refs_1_ = f32[4,1408]{1,0:T(4,128)S(1)} collective-permute-done((f32[4,1408]{1,0:T(4,128)S(1)}, f32[4,1408]{1,0:T(4,128)S(1)}, u32[]{:S(2)}, u32[]{:S(2)}) %collective-permute-start.13) | collective-permute-done | bytes 22560 | tf_op jit(solution)/shard_map/ppermute | solution.py:164
  112.5 1.9 %copy-done.3 = bf16[768,2048]{1,0:T(8,128)(2,1)S(1)} copy-done((bf16[768,2048]{1,0:T(8,128)(2,1)S(1)}, bf16[768,2048]{1,0:T(8,128)(2,1)}, u32[]{:S(2)}) %copy-start.3) | copy-done | bytes 3145752
  114.9 2.1 %collective-permute-start.20 = (f32[4,2048]{1,0:T(4,128)S(1)}, f32[4,2048]{1,0:T(4,128)S(1)}, u32[]{:S(2)}, u32[]{:S(2)}) collective-permute-start(f32[4,2048]{1,0:T(4,128)S(1)} %shard_map.62), channel_id=1, source_target_pairs={{0,8},{8,0},{16,24},{24,16},{32,40},{40,32},{48,56},{56,48},{64,72... | collective-permute-start | bytes 98312 | tf_op jit(solution)/shard_map/ppermute | solution.py:164
  116.9 1.2 collective-permute-done.20
  118.1 2.4 %collective-permute-start.23 = (f32[4,2048]{1,0:T(4,128)S(1)}, f32[4,2048]{1,0:T(4,128)S(1)}, u32[]{:S(2)}, u32[]{:S(2)}) collective-permute-start(f32[4,2048]{1,0:T(4,128)S(1)} %add.32), channel_id=1, source_target_pairs={{0,48},{8,56},{16,32},{24,40},{32,16},{40,24},{48,0},{56,8},{64,11... | collective-permute-start | bytes 98312 | tf_op jit(solution)/shard_map/ppermute | solution.py:164
  120.6 5.8 %collective-permute-start.22 = (f32[4,2048]{1,0:T(4,128)S(1)}, f32[4,2048]{1,0:T(4,128)S(1)}, u32[]{:S(2)}, u32[]{:S(2)}) collective-permute-start(f32[4,2048]{1,0:T(4,128)S(1)} %add.32), channel_id=1, source_target_pairs={{0,32},{8,40},{16,48},{24,56},{32,0},{40,8},{48,16},{56,24},{64,96... | collective-permute-start | bytes 98312 | tf_op jit(solution)/shard_map/ppermute | solution.py:164
  126.4 1.9 %collective-permute-start.21 = (f32[4,2048]{1,0:T(4,128)S(1)}, f32[4,2048]{1,0:T(4,128)S(1)}, u32[]{:S(2)}, u32[]{:S(2)}) collective-permute-start(f32[4,2048]{1,0:T(4,128)S(1)} %add.32), channel_id=1, source_target_pairs={{0,16},{8,24},{16,0},{24,8},{32,48},{40,56},{48,32},{56,40},{64,80... | collective-permute-start | bytes 98312 | tf_op jit(solution)/shard_map/ppermute | solution.py:164
  128.4 3.9 %collective-permute-done.21 = f32[4,2048]{1,0:T(4,128)S(1)} collective-permute-done((f32[4,2048]{1,0:T(4,128)S(1)}, f32[4,2048]{1,0:T(4,128)S(1)}, u32[]{:S(2)}, u32[]{:S(2)}) %collective-permute-start.21) | collective-permute-done | bytes 32800 | tf_op jit(solution)/shard_map/ppermute | solution.py:164
  132.3 5.2 %collective-permute-start.30 = (f32[4,2048]{1,0:T(4,128)S(1)}, f32[4,2048]{1,0:T(4,128)S(1)}, u32[]{:S(2)}, u32[]{:S(2)}) collective-permute-start(f32[4,2048]{1,0:T(4,128)S(1)} %add_add_fusion.refs_0_), channel_id=1, source_target_pairs={{0,448},{8,456},{16,464},{24,472},{32,480},{40,488},{48,496},{56,5... | collective-permute-start | bytes 98312 | tf_op jit(solution)/shard_map/ppermute | solution.py:164
  137.4 3.6 %collective-permute-start.29 = (f32[4,2048]{1,0:T(4,128)S(1)}, f32[4,2048]{1,0:T(4,128)S(1)}, u32[]{:S(2)}, u32[]{:S(2)}) collective-permute-start(f32[4,2048]{1,0:T(4,128)S(1)} %add_add_fusion.refs_0_), channel_id=1, source_target_pairs={{0,384},{8,392},{16,400},{24,408},{32,416},{40,424},{48,432},{56,4... | collective-permute-start | bytes 98312 | tf_op jit(solution)/shard_map/ppermute | solution.py:164
  141.0 5.8 %collective-permute-start.28 = (f32[4,2048]{1,0:T(4,128)S(1)}, f32[4,2048]{1,0:T(4,128)S(1)}, u32[]{:S(2)}, u32[]{:S(2)}) collective-permute-start(f32[4,2048]{1,0:T(4,128)S(1)} %add_add_fusion.refs_0_), channel_id=1, source_target_pairs={{0,320},{8,328},{16,336},{24,344},{32,352},{40,360},{48,368},{56,3... | collective-permute-start | bytes 98312 | tf_op jit(solution)/shard_map/ppermute | solution.py:164
  146.8 3.0 %collective-permute-start.27 = (f32[4,2048]{1,0:T(4,128)S(1)}, f32[4,2048]{1,0:T(4,128)S(1)}, u32[]{:S(2)}, u32[]{:S(2)}) collective-permute-start(f32[4,2048]{1,0:T(4,128)S(1)} %add_add_fusion.refs_0_), channel_id=1, source_target_pairs={{0,256},{8,264},{16,272},{24,280},{32,288},{40,296},{48,304},{56,3... | collective-permute-start | bytes 98312 | tf_op jit(solution)/shard_map/ppermute | solution.py:164
  149.9 4.5 %collective-permute-start.26 = (f32[4,2048]{1,0:T(4,128)S(1)}, f32[4,2048]{1,0:T(4,128)S(1)}, u32[]{:S(2)}, u32[]{:S(2)}) collective-permute-start(f32[4,2048]{1,0:T(4,128)S(1)} %add_add_fusion.refs_0_), channel_id=1, source_target_pairs={{0,192},{8,200},{16,208},{24,216},{32,224},{40,232},{48,240},{56,2... | collective-permute-start | bytes 98312 | tf_op jit(solution)/shard_map/ppermute | solution.py:164
  154.4 2.3 %collective-permute-start.25 = (f32[4,2048]{1,0:T(4,128)S(1)}, f32[4,2048]{1,0:T(4,128)S(1)}, u32[]{:S(2)}, u32[]{:S(2)}) collective-permute-start(f32[4,2048]{1,0:T(4,128)S(1)} %add_add_fusion.refs_0_), channel_id=1, source_target_pairs={{0,128},{8,136},{16,144},{24,152},{32,160},{40,168},{48,176},{56,1... | collective-permute-start | bytes 98312 | tf_op jit(solution)/shard_map/ppermute | solution.py:164
  156.7 3.4 %collective-permute-start.24 = (f32[4,2048]{1,0:T(4,128)S(1)}, f32[4,2048]{1,0:T(4,128)S(1)}, u32[]{:S(2)}, u32[]{:S(2)}) collective-permute-start(f32[4,2048]{1,0:T(4,128)S(1)} %add_add_fusion.refs_0_), channel_id=1, source_target_pairs={{0,64},{8,72},{16,80},{24,88},{32,96},{40,104},{48,112},{56,120},{... | collective-permute-start | bytes 98312 | tf_op jit(solution)/shard_map/ppermute | solution.py:164
  160.1 1.3 shard_map.61
  161.4 1.1 collective-permute-done.24.refs_1_
  162.5 5.1 %shard_map.63 = (f32[4,2048]{1,0:T(4,128)}, bf16[1,640,2048]{2,1,0:T(8,128)(2,1)}) custom-call(f32[4,2048]{1,0:T(4,128)S(1)} %add_add_fusion.refs_0_, f32[4,2048]{1,0:T(4,128)S(1)} %collective-permute-done.24.refs_1_, f32[4,2048]{1,0:T(4,128)S(1)} %collective-permute-done.25.refs_2_, f32[4,2048]{1,0:T(4,128)S(1)} %collective-permute-done.26.refs_3_, ...), custom_call_target="tpu_custom_call" | custom-call | flops 2013265920 | bytes 7135232 | tf_op jit(solution)/shard_map/pallas_call | solution.py:151
  (44 shorter events, 2.9 us)
Async XLA Ops:
  7.2 105.3 %all-gather.2.cloned.1.call-start = ((), (), s32[]{:S(2)}) async-start(), calls=%async_computation | async-start | bytes 3538944 | tf_op jit(solution)/shard_map/all_gather | solution.py:177
  7.9 1.0 copy-start.5
  8.9 0.8 copy-start.6
  9.9 26.1 %collective-permute-start.6 = (f32[4,768]{1,0:T(4,128)S(1)}, f32[4,768]{1,0:T(4,128)S(1)}, u32[]{:S(2)}, u32[]{:S(2)}) collective-permute-start(f32[4,768]{1,0:T(4,128)S(1)} %shard_map.58.refs_0_), channel_id=1, source_target_pairs={{0,7},{1,6},{2,5},{3,4},{4,3},{5,2},{6,1},{7,0},{8,15},{9,14},{10,... | collective-permute-start | bytes 36872 | tf_op jit(solution)/shard_map/ppermute | solution.py:164
  20.9 17.6 %collective-permute-start.5 = (f32[4,768]{1,0:T(4,128)S(1)}, f32[4,768]{1,0:T(4,128)S(1)}, u32[]{:S(2)}, u32[]{:S(2)}) collective-permute-start(f32[4,768]{1,0:T(4,128)S(1)} %shard_map.58.refs_0_), channel_id=1, source_target_pairs={{0,6},{1,7},{2,4},{3,5},{4,2},{5,3},{6,0},{7,1},{8,14},{9,15},{10,... | collective-permute-start | bytes 36872 | tf_op jit(solution)/shard_map/ppermute | solution.py:164
  22.8 19.9 %collective-permute-start.4 = (f32[4,768]{1,0:T(4,128)S(1)}, f32[4,768]{1,0:T(4,128)S(1)}, u32[]{:S(2)}, u32[]{:S(2)}) collective-permute-start(f32[4,768]{1,0:T(4,128)S(1)} %shard_map.58.refs_0_), channel_id=1, source_target_pairs={{0,5},{1,4},{2,7},{3,6},{4,1},{5,0},{6,3},{7,2},{8,13},{9,12},{10,... | collective-permute-start | bytes 36872 | tf_op jit(solution)/shard_map/ppermute | solution.py:164
  27.9 14.8 %collective-permute-start.3 = (f32[4,768]{1,0:T(4,128)S(1)}, f32[4,768]{1,0:T(4,128)S(1)}, u32[]{:S(2)}, u32[]{:S(2)}) collective-permute-start(f32[4,768]{1,0:T(4,128)S(1)} %shard_map.58.refs_0_), channel_id=1, source_target_pairs={{0,4},{1,5},{2,6},{3,7},{4,0},{5,1},{6,2},{7,3},{8,12},{9,13},{10,... | collective-permute-start | bytes 36872 | tf_op jit(solution)/shard_map/ppermute | solution.py:164
  32.6 10.2 %collective-permute-start.2 = (f32[4,768]{1,0:T(4,128)S(1)}, f32[4,768]{1,0:T(4,128)S(1)}, u32[]{:S(2)}, u32[]{:S(2)}) collective-permute-start(f32[4,768]{1,0:T(4,128)S(1)} %shard_map.58.refs_0_), channel_id=1, source_target_pairs={{0,3},{1,2},{2,1},{3,0},{4,7},{5,6},{6,5},{7,4},{8,11},{9,10},{10,... | collective-permute-start | bytes 36872 | tf_op jit(solution)/shard_map/ppermute | solution.py:164
  35.9 6.8 %collective-permute-start.1 = (f32[4,768]{1,0:T(4,128)S(1)}, f32[4,768]{1,0:T(4,128)S(1)}, u32[]{:S(2)}, u32[]{:S(2)}) collective-permute-start(f32[4,768]{1,0:T(4,128)S(1)} %shard_map.58.refs_0_), channel_id=1, source_target_pairs={{0,2},{1,3},{2,0},{3,1},{4,6},{5,7},{6,4},{7,5},{8,10},{9,11},{10,... | collective-permute-start | bytes 36872 | tf_op jit(solution)/shard_map/ppermute | solution.py:164
  38.4 5.9 %collective-permute-start = (f32[4,768]{1,0:T(4,128)S(1)}, f32[4,768]{1,0:T(4,128)S(1)}, u32[]{:S(2)}, u32[]{:S(2)}) collective-permute-start(f32[4,768]{1,0:T(4,128)S(1)} %shard_map.58.refs_0_), channel_id=1, source_target_pairs={{0,1},{1,0},{2,3},{3,2},{4,5},{5,4},{6,7},{7,6},{8,9},{9,8},{10,11... | collective-permute-start | bytes 36872 | tf_op jit(solution)/shard_map/ppermute | solution.py:164
  44.4 1.2 copy-start
  45.6 116.9 %copy-start.2 = (bf16[768,640]{1,0:T(8,128)(2,1)S(1)}, bf16[768,640]{1,0:T(8,128)(2,1)}, u32[]{:S(2)}) copy-start(bf16[768,640]{1,0:T(8,128)(2,1)} %refs_8_.3) | copy-start | bytes 2949124
  45.8 3.2 %collective-permute-start.7 = (f32[4,640]{1,0:T(4,128)S(1)}, f32[4,640]{1,0:T(4,128)S(1)}, u32[]{:S(2)}, u32[]{:S(2)}) collective-permute-start(f32[4,640]{1,0:T(4,128)S(1)} %shard_map.59), channel_id=1, source_target_pairs={{0,8},{8,0},{16,24},{24,16},{32,40},{40,32},{48,56},{56,48},{64,72... | collective-permute-start | bytes 30728 | tf_op jit(solution)/shard_map/ppermute | solution.py:164
  49.1 5.6 %collective-permute-start.8 = (f32[4,640]{1,0:T(4,128)S(1)}, f32[4,640]{1,0:T(4,128)S(1)}, u32[]{:S(2)}, u32[]{:S(2)}) collective-permute-start(f32[4,640]{1,0:T(4,128)S(1)} %add.27), channel_id=1, source_target_pairs={{0,16},{8,24},{16,0},{24,8},{32,48},{40,56},{48,32},{56,40},{64,80... | collective-permute-start | bytes 30728 | tf_op jit(solution)/shard_map/ppermute | solution.py:164
  54.6 5.6 %collective-permute-start.9 = (f32[4,640]{1,0:T(4,128)S(1)}, f32[4,640]{1,0:T(4,128)S(1)}, u32[]{:S(2)}, u32[]{:S(2)}) collective-permute-start(f32[4,640]{1,0:T(4,128)S(1)} %add.28), channel_id=1, source_target_pairs={{0,48},{8,56},{16,32},{24,40},{32,16},{40,24},{48,0},{56,8},{64,11... | collective-permute-start | bytes 30728 | tf_op jit(solution)/shard_map/ppermute | solution.py:164
  60.2 5.6 %collective-permute-start.10 = (f32[4,640]{1,0:T(4,128)S(1)}, f32[4,640]{1,0:T(4,128)S(1)}, u32[]{:S(2)}, u32[]{:S(2)}) collective-permute-start(f32[4,640]{1,0:T(4,128)S(1)} %add.29), channel_id=1, source_target_pairs={{0,64},{8,72},{16,80},{24,88},{32,96},{40,104},{48,112},{56,120},{... | collective-permute-start | bytes 30728 | tf_op jit(solution)/shard_map/ppermute | solution.py:164
  65.7 6.5 %collective-permute-start.11 = (f32[4,640]{1,0:T(4,128)S(1)}, f32[4,640]{1,0:T(4,128)S(1)}, u32[]{:S(2)}, u32[]{:S(2)}) collective-permute-start(f32[4,640]{1,0:T(4,128)S(1)} %add.30), channel_id=1, source_target_pairs={{0,128},{8,136},{16,144},{24,152},{32,160},{40,168},{48,176},{56,1... | collective-permute-start | bytes 30728 | tf_op jit(solution)/shard_map/ppermute | solution.py:164
  72.2 7.9 %collective-permute-start.12 = (f32[4,640]{1,0:T(4,128)S(1)}, f32[4,640]{1,0:T(4,128)S(1)}, u32[]{:S(2)}, u32[]{:S(2)}) collective-permute-start(f32[4,640]{1,0:T(4,128)S(1)} %add.31.refs_0_), channel_id=1, source_target_pairs={{0,384},{8,392},{16,400},{24,408},{32,416},{40,424},{48,432},{56,4... | collective-permute-start | bytes 30728 | tf_op jit(solution)/shard_map/ppermute | solution.py:164
  80.1 1.2 copy-start.1
  81.7 21.8 %collective-permute-start.19 = (f32[4,1408]{1,0:T(4,128)S(1)}, f32[4,1408]{1,0:T(4,128)S(1)}, u32[]{:S(2)}, u32[]{:S(2)}) collective-permute-start(f32[4,1408]{1,0:T(4,128)S(1)} %shard_map.60.refs_0_), channel_id=1, source_target_pairs={{0,7},{1,6},{2,5},{3,4},{4,3},{5,2},{6,1},{7,0},{8,15},{9,14},{10,... | collective-permute-start | bytes 67592 | tf_op jit(solution)/shard_map/ppermute | solution.py:164
  87.4 19.4 %collective-permute-start.18 = (f32[4,1408]{1,0:T(4,128)S(1)}, f32[4,1408]{1,0:T(4,128)S(1)}, u32[]{:S(2)}, u32[]{:S(2)}) collective-permute-start(f32[4,1408]{1,0:T(4,128)S(1)} %shard_map.60.refs_0_), channel_id=1, source_target_pairs={{0,6},{1,7},{2,4},{3,5},{4,2},{5,3},{6,0},{7,1},{8,14},{9,15},{10,... | collective-permute-start | bytes 67592 | tf_op jit(solution)/shard_map/ppermute | solution.py:164
  91.1 19.1 %collective-permute-start.17 = (f32[4,1408]{1,0:T(4,128)S(1)}, f32[4,1408]{1,0:T(4,128)S(1)}, u32[]{:S(2)}, u32[]{:S(2)}) collective-permute-start(f32[4,1408]{1,0:T(4,128)S(1)} %shard_map.60.refs_0_), channel_id=1, source_target_pairs={{0,5},{1,4},{2,7},{3,6},{4,1},{5,0},{6,3},{7,2},{8,13},{9,12},{10,... | collective-permute-start | bytes 67592 | tf_op jit(solution)/shard_map/ppermute | solution.py:164
  95.3 14.9 %collective-permute-start.16 = (f32[4,1408]{1,0:T(4,128)S(1)}, f32[4,1408]{1,0:T(4,128)S(1)}, u32[]{:S(2)}, u32[]{:S(2)}) collective-permute-start(f32[4,1408]{1,0:T(4,128)S(1)} %shard_map.60.refs_0_), channel_id=1, source_target_pairs={{0,4},{1,5},{2,6},{3,7},{4,0},{5,1},{6,2},{7,3},{8,12},{9,13},{10,... | collective-permute-start | bytes 67592 | tf_op jit(solution)/shard_map/ppermute | solution.py:164
  100.0 10.2 %collective-permute-start.15 = (f32[4,1408]{1,0:T(4,128)S(1)}, f32[4,1408]{1,0:T(4,128)S(1)}, u32[]{:S(2)}, u32[]{:S(2)}) collective-permute-start(f32[4,1408]{1,0:T(4,128)S(1)} %shard_map.60.refs_0_), channel_id=1, source_target_pairs={{0,3},{1,2},{2,1},{3,0},{4,7},{5,6},{6,5},{7,4},{8,11},{9,10},{10,... | collective-permute-start | bytes 67592 | tf_op jit(solution)/shard_map/ppermute | solution.py:164
  103.4 6.8 %collective-permute-start.14 = (f32[4,1408]{1,0:T(4,128)S(1)}, f32[4,1408]{1,0:T(4,128)S(1)}, u32[]{:S(2)}, u32[]{:S(2)}) collective-permute-start(f32[4,1408]{1,0:T(4,128)S(1)} %shard_map.60.refs_0_), channel_id=1, source_target_pairs={{0,2},{1,3},{2,0},{3,1},{4,6},{5,7},{6,4},{7,5},{8,10},{9,11},{10,... | collective-permute-start | bytes 67592 | tf_op jit(solution)/shard_map/ppermute | solution.py:164
  106.7 5.7 %collective-permute-start.13 = (f32[4,1408]{1,0:T(4,128)S(1)}, f32[4,1408]{1,0:T(4,128)S(1)}, u32[]{:S(2)}, u32[]{:S(2)}) collective-permute-start(f32[4,1408]{1,0:T(4,128)S(1)} %shard_map.60.refs_0_), channel_id=1, source_target_pairs={{0,1},{1,0},{2,3},{3,2},{4,5},{5,4},{6,7},{7,6},{8,9},{9,8},{10,11... | collective-permute-start | bytes 67592 | tf_op jit(solution)/shard_map/ppermute | solution.py:164
  112.4 1.9 %copy-start.3 = (bf16[768,2048]{1,0:T(8,128)(2,1)S(1)}, bf16[768,2048]{1,0:T(8,128)(2,1)}, u32[]{:S(2)}) copy-start(bf16[768,2048]{1,0:T(8,128)(2,1)} %all-gather.2.cloned.1.call-done.refs_8_.refs_9_) | copy-start | bytes 9437188
  114.3 48.1 %copy-start.4 = (bf16[768,2048]{1,0:T(8,128)(2,1)S(1)}, bf16[768,2048]{1,0:T(8,128)(2,1)}, u32[]{:S(2)}) copy-start(bf16[768,2048]{1,0:T(8,128)(2,1)} %all-gather.2.cloned.1.call-done.refs_8_.refs_9_) | copy-start | bytes 9437188
  114.9 3.2 %collective-permute-start.20 = (f32[4,2048]{1,0:T(4,128)S(1)}, f32[4,2048]{1,0:T(4,128)S(1)}, u32[]{:S(2)}, u32[]{:S(2)}) collective-permute-start(f32[4,2048]{1,0:T(4,128)S(1)} %shard_map.62), channel_id=1, source_target_pairs={{0,8},{8,0},{16,24},{24,16},{32,40},{40,32},{48,56},{56,48},{64,72... | collective-permute-start | bytes 98312 | tf_op jit(solution)/shard_map/ppermute | solution.py:164
  118.1 10.2 %collective-permute-start.23 = (f32[4,2048]{1,0:T(4,128)S(1)}, f32[4,2048]{1,0:T(4,128)S(1)}, u32[]{:S(2)}, u32[]{:S(2)}) collective-permute-start(f32[4,2048]{1,0:T(4,128)S(1)} %add.32), channel_id=1, source_target_pairs={{0,48},{8,56},{16,32},{24,40},{32,16},{40,24},{48,0},{56,8},{64,11... | collective-permute-start | bytes 98312 | tf_op jit(solution)/shard_map/ppermute | solution.py:164
  120.6 7.8 %collective-permute-start.22 = (f32[4,2048]{1,0:T(4,128)S(1)}, f32[4,2048]{1,0:T(4,128)S(1)}, u32[]{:S(2)}, u32[]{:S(2)}) collective-permute-start(f32[4,2048]{1,0:T(4,128)S(1)} %add.32), channel_id=1, source_target_pairs={{0,32},{8,40},{16,48},{24,56},{32,0},{40,8},{48,16},{56,24},{64,96... | collective-permute-start | bytes 98312 | tf_op jit(solution)/shard_map/ppermute | solution.py:164
  126.4 5.8 %collective-permute-start.21 = (f32[4,2048]{1,0:T(4,128)S(1)}, f32[4,2048]{1,0:T(4,128)S(1)}, u32[]{:S(2)}, u32[]{:S(2)}) collective-permute-start(f32[4,2048]{1,0:T(4,128)S(1)} %add.32), channel_id=1, source_target_pairs={{0,16},{8,24},{16,0},{24,8},{32,48},{40,56},{48,32},{56,40},{64,80... | collective-permute-start | bytes 98312 | tf_op jit(solution)/shard_map/ppermute | solution.py:164
  132.3 22.1 %collective-permute-start.30 = (f32[4,2048]{1,0:T(4,128)S(1)}, f32[4,2048]{1,0:T(4,128)S(1)}, u32[]{:S(2)}, u32[]{:S(2)}) collective-permute-start(f32[4,2048]{1,0:T(4,128)S(1)} %add_add_fusion.refs_0_), channel_id=1, source_target_pairs={{0,448},{8,456},{16,464},{24,472},{32,480},{40,488},{48,496},{56,5... | collective-permute-start | bytes 98312 | tf_op jit(solution)/shard_map/ppermute | solution.py:164
  137.4 19.2 %collective-permute-start.29 = (f32[4,2048]{1,0:T(4,128)S(1)}, f32[4,2048]{1,0:T(4,128)S(1)}, u32[]{:S(2)}, u32[]{:S(2)}) collective-permute-start(f32[4,2048]{1,0:T(4,128)S(1)} %add_add_fusion.refs_0_), channel_id=1, source_target_pairs={{0,384},{8,392},{16,400},{24,408},{32,416},{40,424},{48,432},{56,4... | collective-permute-start | bytes 98312 | tf_op jit(solution)/shard_map/ppermute | solution.py:164
  141.0 20.4 %collective-permute-start.28 = (f32[4,2048]{1,0:T(4,128)S(1)}, f32[4,2048]{1,0:T(4,128)S(1)}, u32[]{:S(2)}, u32[]{:S(2)}) collective-permute-start(f32[4,2048]{1,0:T(4,128)S(1)} %add_add_fusion.refs_0_), channel_id=1, source_target_pairs={{0,320},{8,328},{16,336},{24,344},{32,352},{40,360},{48,368},{56,3... | collective-permute-start | bytes 98312 | tf_op jit(solution)/shard_map/ppermute | solution.py:164
  146.8 14.5 %collective-permute-start.27 = (f32[4,2048]{1,0:T(4,128)S(1)}, f32[4,2048]{1,0:T(4,128)S(1)}, u32[]{:S(2)}, u32[]{:S(2)}) collective-permute-start(f32[4,2048]{1,0:T(4,128)S(1)} %add_add_fusion.refs_0_), channel_id=1, source_target_pairs={{0,256},{8,264},{16,272},{24,280},{32,288},{40,296},{48,304},{56,3... | collective-permute-start | bytes 98312 | tf_op jit(solution)/shard_map/ppermute | solution.py:164
  149.9 11.5 %collective-permute-start.26 = (f32[4,2048]{1,0:T(4,128)S(1)}, f32[4,2048]{1,0:T(4,128)S(1)}, u32[]{:S(2)}, u32[]{:S(2)}) collective-permute-start(f32[4,2048]{1,0:T(4,128)S(1)} %add_add_fusion.refs_0_), channel_id=1, source_target_pairs={{0,192},{8,200},{16,208},{24,216},{32,224},{40,232},{48,240},{56,2... | collective-permute-start | bytes 98312 | tf_op jit(solution)/shard_map/ppermute | solution.py:164
  154.4 7.0 %collective-permute-start.25 = (f32[4,2048]{1,0:T(4,128)S(1)}, f32[4,2048]{1,0:T(4,128)S(1)}, u32[]{:S(2)}, u32[]{:S(2)}) collective-permute-start(f32[4,2048]{1,0:T(4,128)S(1)} %add_add_fusion.refs_0_), channel_id=1, source_target_pairs={{0,128},{8,136},{16,144},{24,152},{32,160},{40,168},{48,176},{56,1... | collective-permute-start | bytes 98312 | tf_op jit(solution)/shard_map/ppermute | solution.py:164
  156.7 5.8 %collective-permute-start.24 = (f32[4,2048]{1,0:T(4,128)S(1)}, f32[4,2048]{1,0:T(4,128)S(1)}, u32[]{:S(2)}, u32[]{:S(2)}) collective-permute-start(f32[4,2048]{1,0:T(4,128)S(1)} %add_add_fusion.refs_0_), channel_id=1, source_target_pairs={{0,64},{8,72},{16,80},{24,88},{32,96},{40,104},{48,112},{56,120},{... | collective-permute-start | bytes 98312 | tf_op jit(solution)/shard_map/ppermute | solution.py:164
Sparse Core Ops, SparseCore 0:
  10.0 65.4 all-gather.1

commit v2 on v1

--- a/solution.py
+++ b/solution.py
@@ -6,11 +6,12 @@
 from jax import lax
 from jax.experimental import pallas as pl
 from jax.experimental.pallas import tpu as pltpu
+from jax.sharding import Mesh
 from jax.sharding import PartitionSpec as P
 
 F32 = jnp.float32
 BF16 = jnp.bfloat16
-VMEM_BYTES = 40 * 1024 * 1024
+VMEM_BYTES = 24 * 1024 * 1024
 PIECE_PAIRS = ((0, 0), (0, 1), (1, 0), (0, 2), (1, 1), (2, 0))
 
 
@@ -22,11 +23,8 @@
     return high, middle, low
 
 
-def tree_sum(values):
-    values = list(values)
-    while len(values) > 1:
-        values = [values[i] + values[i + 1] for i in range(0, len(values), 2)]
-    return values[0]
+def spread(out_ref, value):
+    out_ref[...] = jnp.broadcast_to(value[None], out_ref.shape)
 
 
 def fold(product, rank):
@@ -48,47 +46,48 @@
     product = lax.dot_general(
         rows, grads_ref[...], (((1,), (1,)), ((), ())), preferred_element_type=F32
     )
-    out_ref[...] = fold(product, prev_ref.shape[0])
-
-
-def left_kernel(*refs):
-    *parts, acts_ref, out_ref, stack = refs
-    rows = stack_pieces(tree_sum([p[...] for p in parts]), stack)
+    spread(out_ref, fold(product, prev_ref.shape[0]))
+
+
+def left_kernel(parts_ref, acts_ref, out_ref, stack):
+    rows = stack_pieces(jnp.sum(parts_ref[...], axis=0), stack)
     product = jnp.dot(rows, acts_ref[...], preferred_element_type=F32)
-    out_ref[...] = fold(product, out_ref.shape[0])
-
-
-def back_kernel(scale, *refs):
-    *parts, acts_ref, out_ref, stack = refs
+    spread(out_ref, fold(product, parts_ref.shape[1]))
+
+
+def sum_kernel(parts_ref, out_ref):
+    spread(out_ref, jnp.sum(parts_ref[...], axis=0))
+
+
+def back_kernel(scale, parts_ref, acts_ref, out_ref, stack):
     units = acts_ref.shape[1]
-    raw = tree_sum([p[...] for p in parts]) * scale
+    raw = jnp.sum(parts_ref[...], axis=0) * scale
     rows = stack_pieces(raw, stack)
     product = lax.dot_general(
         rows, acts_ref[...], (((1,), (1,)), ((), ())), preferred_element_type=F32
     )
-    out_ref[:, :units] = raw
-    out_ref[:, units:] = fold(product, out_ref.shape[0])
-
-
-def right_kernel(units, *refs):
-    *parts, grads_ref, out_ref, stack = refs
-    rows = stack_pieces(tree_sum([p[:, units:] for p in parts]), stack)
+    ways = out_ref.shape[0]
+    out_ref[:, :, :units] = jnp.broadcast_to(raw[None], (ways, *raw.shape))
+    result = fold(product, raw.shape[0])
+    out_ref[:, :, units:] = jnp.broadcast_to(result[None], (ways, *result.shape))
+
+
+def right_kernel(units, parts_ref, grads_ref, out_ref, stack):
+    rows = stack_pieces(jnp.sum(parts_ref[:, :, units:], axis=0), stack)
     product = jnp.dot(rows, grads_ref[...], preferred_element_type=F32)
-    out_ref[...] = fold(product, out_ref.shape[0])
+    spread(out_ref, fold(product, parts_ref.shape[1]))
 
 
 def total(x):
     return jnp.sum(jnp.sum(x, axis=1, keepdims=True), axis=0, keepdims=True)
 
 
-def basis_kernel(units, full_units, *refs):
-    *parts, basis_ref, wide_ref, map_ref, rows, unit = refs
-    rank = basis_ref.shape[0]
+def basis_kernel(units, full_units, parts_ref, basis_ref, wide_ref, map_ref, rows, unit):
+    ways, rank, _ = parts_ref.shape
     me = lax.axis_index("mp")
-    for k, part in enumerate(parts):
-        place = jnp.bitwise_xor(me, k)
+    for k in range(ways):
         for r in range(rank):
-            rows[r, pl.ds(place, 1), :] = part[r:r + 1, :units]
+            rows[r, k:k + 1, :] = parts_ref[k, r:r + 1, :units]
     units_done, maps = [], []
     for k in range(rank):
         raw = rows[k]
@@ -118,13 +117,14 @@
             wide_ref[rank * i + k:rank * i + k + 1, :] = split[a]
 
 
-def residual_kernel(scale, *refs):
-    *parts, acts_ref, grads_ref, wide_ref, map_ref, factor_ref, out_ref, held = refs
-    rank = factor_ref.shape[0]
+def residual_kernel(
+    scale, parts_ref, acts_ref, grads_ref, wide_ref, map_ref, factor_ref, out_ref, held
+):
+    ways, rank, _ = parts_ref.shape
 
     @pl.when(pl.program_id(0) == 0)
     def _():
-        y = tree_sum([p[...] for p in parts]) * scale
+        y = jnp.concatenate([parts_ref[i] for i in range(ways)], axis=1) * scale
         held[...] = jnp.zeros_like(held)
         for k in range(rank):
             line = functools.reduce(
@@ -158,66 +158,61 @@
     )(*args)
 
 
-def exchange(x, axis, masks):
-    size = lax.axis_size(axis)
-    return [
-        x if mask == 0 else lax.ppermute(x, axis, [(i, i ^ mask) for i in range(size)])
-        for mask in masks
-    ]
+def exchange(copies, axis):
+    return lax.all_to_all(copies, axis, 0, 0, tiled=True)
 
 
 def local(hidden_acts, out_grads, prev_factor):
     tokens, units = hidden_acts.shape
     rank, width = prev_factor.shape
-    replicas = lax.axis_size("dp")
-    ways = lax.axis_size("mp")
+    ways, near, far = (lax.axis_size(a) for a in ("mp", "near", "far"))
+    replicas = near * far
+    part = width // ways
     rows = lambda n: pltpu.VMEM((16, n), F32)
     shape = lambda *dims: jax.ShapeDtypeStruct(dims, F32)
 
     grads = lax.all_gather(out_grads, "mp", axis=1, tiled=True)
 
     coeffs = call(
-        coeff_kernel, [shape(rank, tokens)], [prev_factor, out_grads],
-        [rows(out_grads.shape[1])], 32 * tokens * out_grads.shape[1],
-    )
-    coeffs = exchange(coeffs, "mp", range(ways))
+        coeff_kernel, [shape(ways, rank, tokens)], [prev_factor, out_grads],
+        [rows(part)], 32 * tokens * part,
+    )
     left = call(
-        left_kernel, [shape(rank, units)], [*coeffs, hidden_acts],
+        left_kernel, [shape(near, rank, units)], [exchange(coeffs, "mp"), hidden_acts],
         [rows(tokens)], 32 * tokens * units,
     )
-    for mask in (1, 2, 6, 8, 16):
-        left = tree_sum(exchange(left, "dp", (0, mask)))
+    left = call(sum_kernel, [shape(far, rank, units)], [exchange(left, "near")], [], 8 * units)
     packed = call(
-        functools.partial(back_kernel, 1.0 / replicas), [shape(rank, units + tokens)],
-        [*exchange(left, "dp", (0, 48)), hidden_acts],
-        [rows(units)], 32 * tokens * units,
-    )
-    packed = exchange(packed, "mp", range(ways))
+        functools.partial(back_kernel, 1.0 / replicas), [shape(ways, rank, units + tokens)],
+        [exchange(left, "far"), hidden_acts], [rows(units)], 32 * tokens * units,
+    )
+    packed = exchange(packed, "mp")
     right = call(
-        functools.partial(right_kernel, units), [shape(rank, width)], [*packed, grads],
-        [rows(tokens)], 32 * tokens * width,
+        functools.partial(right_kernel, units), [shape(near, rank, part)],
+        [packed, out_grads], [rows(tokens)], 32 * tokens * part,
     )
     basis, wide, maps = call(
         functools.partial(basis_kernel, units, units * ways),
-        [shape(rank, units), shape(32, units), shape(rank * rank, 128)], packed,
+        [shape(rank, units), shape(32, units), shape(rank * rank, 128)], [packed],
         [pltpu.VMEM((rank, ways, units), F32), pltpu.VMEM((rank, ways, units), F32)],
         100 * ways * units,
     )
-    right = tree_sum(exchange(right, "dp", (0, 1)))
-    right = tree_sum(exchange(right, "dp", (0, 2, 4, 6)))
-    right = exchange(right, "dp", range(0, 64, 8))
+    right = call(sum_kernel, [shape(far, rank, part)], [exchange(right, "near")], [], 8 * part)
+    right = call(sum_kernel, [shape(ways, rank, part)], [exchange(right, "far")], [], 8 * part)
+    right = exchange(right, "mp")
 
     tile = 128
     whole = lambda *dims: pl.BlockSpec(dims, lambda i: (0,) * len(dims))
     factor, residual = call(
         functools.partial(residual_kernel, 1.0 / replicas),
         [shape(rank, width), jax.ShapeDtypeStruct((1, units, width), BF16)],
-        [*right, hidden_acts, grads, wide, maps],
+        [right, hidden_acts, grads, wide, maps],
         [pltpu.VMEM((32, width), F32)],
         2 * tokens * units * width,
         dict(
             grid=(units // tile,),
-            in_specs=[whole(rank, width)] * len(right) + [
+            in_specs=[
+                whole(ways, rank, part),
                 pl.BlockSpec((tokens, tile), lambda i: (0, i)),
                 whole(tokens, width),
                 pl.BlockSpec((32, tile), lambda i: (0, i)),
@@ -230,10 +225,14 @@
 
 
 def solution(mesh):
+    replicas, ways = mesh.devices.shape
+    far = 8 if replicas % 8 == 0 else 1
+    split = Mesh(mesh.devices.reshape(far, replicas // far, ways), ("far", "near", "mp"))
+    dp = ("far", "near")
     return jax.shard_map(
         local,
-        mesh=mesh,
-        in_specs=(P("dp", "mp"), P("dp", "mp"), P()),
-        out_specs=(P(None, "mp"), P(), P("dp", "mp", None)),
+        mesh=split,
+        in_specs=(P(dp, "mp"), P(dp, "mp"), P()),
+        out_specs=(P(None, "mp"), P(), P(dp, "mp", None)),
         check_vma=False,
     )

time: 176 us -> 113 us (0.64)
  the two profiles are of different devices: /device:TPU:4 before, /device:TPU:1 now
where the time goes in v2:
time: 113 us; the launch traced here: 112 us
  blocking collectives  75.3 us (67%)
  between operations  14.1 us (12%)
  Pallas kernels  8.14 us (7%)
  waiting for transfers between devices  6.18 us (5%)
  local copies, waits for them, and re-layouts  4.85 us (4%)
  starting transfers between devices  3.38 us (3%)
    all_to_all x6, blocking collectives, exchange(): return lax.all_to_all(copies, axis, 0, 0, tiled=True)  75.3 us
    pallas_call x9, Pallas kernels, call(): pl.pallas_call(kernel, out_shape=outs[0] if single else outs, scratch_sha...  8.14 us
    all_to_all x1, waiting for transfers between devices, exchange(): return lax.all_to_all(copies, axis, 0, 0, tiled=True)  5.5 us
    unnamed x12, local copies, waits for them, and re-layouts  4.85 us
    all_to_all x1, starting transfers between devices, exchange(): return lax.all_to_all(copies, axis, 0, 0, tiled=True)  3.34 us
  transfers between devices with their start and end apart: 2, of which 1 were waited for; matrix products, arithmetic and copies ran while one was open for 0% of the time, Pallas kernels for 3%

profile of v2, /device:TPU:1, one launch (start us, length us, event | category | flops | bytes accessed | tf_op | source)
XLA Modules:
  0.0 112.0 jit_solution(15140248070744119808)
XLA Ops:
  7.2 0.0 copy-start.1
  7.2 0.0 all-gather.2.cloned.1.call-start
  7.2 0.7 all-gather.2.cloned.1.call-update
  7.9 0.0 copy-start.2
  7.9 1.0 copy-done.2
  8.9 0.0 copy-start.4
  8.9 0.8 copy-done.4
  9.7 0.3 shard_map.58
  9.9 18.3 %all_to_all.35.parts_ref = f32[8,4,768]{2,1,0:T(4,128)S(1)} all-to-all(f32[8,4,768]{2,1,0:T(4,128)S(1)} %shard_map.58), channel_id=1, replica_groups=mesh['far'=8,'near'=8,'mp'=8] {'mp'}, dimensions={0} | all-to-all | bytes 196608 | tf_op jit(solution)/shard_map/all_to_all | solution.py:162
  28.2 0.0 copy-start
  28.2 1.2 %copy-done = bf16[768,640]{1,0:T(8,128)(2,1)S(1)} copy-done((bf16[768,640]{1,0:T(8,128)(2,1)S(1)}, bf16[768,640]{1,0:T(8,128)(2,1)}, u32[]{:S(2)}) %copy-start) | copy-done | bytes 983064
  29.4 0.0 copy-start.3
  29.4 0.3 shard_map.59
  29.7 11.1 %all_to_all.36.parts_ref = f32[8,4,640]{2,1,0:T(4,128)S(1)} all-to-all(f32[8,4,640]{2,1,0:T(4,128)S(1)} %shard_map.59), channel_id=1, replica_groups=mesh['far'=8,'near'=8,'mp'=8] {'near'}, dimensions={0} | all-to-all | bytes 163840 | tf_op jit(solution)/shard_map/all_to_all | solution.py:162
  40.8 14.1 %all_to_all.37.parts_ref = f32[8,4,640]{2,1,0:T(4,128)S(1)} all-to-all(f32[8,4,640]{2,1,0:T(4,128)S(1)} %shard_map.60), channel_id=1, replica_groups=mesh['far'=8,'near'=8,'mp'=8] {'far'}, dimensions={0} | all-to-all | bytes 163840 | tf_op jit(solution)/shard_map/all_to_all | solution.py:162
  54.9 0.0 copy-done.1
  54.9 0.4 shard_map.61
  55.3 12.9 %all_to_all.38.parts_ref = f32[8,4,1408]{2,1,0:T(4,128)S(1)} all-to-all(f32[8,4,1408]{2,1,0:T(4,128)S(1)} %shard_map.61), channel_id=1, replica_groups=mesh['far'=8,'near'=8,'mp'=8] {'mp'}, dimensions={0} | all-to-all | bytes 360448 | tf_op jit(solution)/shard_map/all_to_all | solution.py:162
  68.2 0.0 copy-done.3
  68.2 0.2 shard_map.63
  68.4 9.7 %all_to_all.39.parts_ref = f32[8,4,256]{2,1,0:T(4,128)S(1)} all-to-all(f32[8,4,256]{2,1,0:T(4,128)S(1)} %shard_map.63), channel_id=1, replica_groups=mesh['far'=8,'near'=8,'mp'=8] {'near'}, dimensions={0} | all-to-all | bytes 65536 | tf_op jit(solution)/shard_map/all_to_all | solution.py:162
  78.1 9.2 %all_to_all.40.parts_ref = f32[8,4,256]{2,1,0:T(4,128)S(1)} all-to-all(f32[8,4,256]{2,1,0:T(4,128)S(1)} %shard_map.64), channel_id=1, replica_groups=mesh['far'=8,'near'=8,'mp'=8] {'far'}, dimensions={0} | all-to-all | bytes 65536 | tf_op jit(solution)/shard_map/all_to_all | solution.py:162
  87.4 0.6 shard_map.65
  88.0 3.3 %all-to-all-start.6 = ((f32[8,4,256]{2,1,0:T(4,128)}), f32[8,4,256]{2,1,0:T(4,128)S(1)}, u32[]{:S(2)}, u32[]{:S(2)}) async-start(f32[8,4,256]{2,1,0:T(4,128)} %shard_map.65), calls=%async_computation.6 | async-start | bytes 65536 | tf_op jit(solution)/shard_map/all_to_all | solution.py:162
  91.3 1.3 %shard_map.62 = (f32[4,640]{1,0:T(4,128)}, f32[32,640]{1,0:T(8,128)S(1)}, f32[16,128]{1,0:T(8,128)S(1)}) custom-call(f32[8,4,1408]{2,1,0:T(4,128)S(1)} %all_to_all.38.parts_ref), custom_call_target="tpu_custom_call" | custom-call | flops 512000 | bytes 280576 | tf_op jit(solution)/shard_map/pallas_call | solution.py:151
  92.6 5.5 %all-to-all-done.6.parts_ref = f32[8,4,256]{2,1,0:T(4,128)S(1)} async-done(((f32[8,4,256]{2,1,0:T(4,128)}), f32[8,4,256]{2,1,0:T(4,128)S(1)}, u32[]{:S(2)}, u32[]{:S(2)}) %all-to-all-start.6) | async-done | bytes 32800 | tf_op jit(solution)/shard_map/all_to_all | solution.py:162
  98.1 0.0 all-gather.2.cloned.1.call-done.grads_ref
  98.1 0.0 copy-start.5
  98.1 1.9 %copy-done.5 = bf16[768,2048]{1,0:T(8,128)(2,1)S(1)} copy-done((bf16[768,2048]{1,0:T(8,128)(2,1)S(1)}, bf16[768,2048]{1,0:T(8,128)(2,1)}, u32[]{:S(2)}) %copy-start.5) | copy-done | bytes 3145752
  100.0 5.1 %shard_map.66 = (f32[4,2048]{1,0:T(4,128)}, bf16[1,640,2048]{2,1,0:T(8,128)(2,1)}) custom-call(f32[8,4,256]{2,1,0:T(4,128)S(1)} %all-to-all-done.6.parts_ref, bf16[768,640]{1,0:T(8,128)(2,1)S(1)} %copy-done.1, bf16[768,2048]{1,0:T(8,128)(2,1)S(1)} %copy-done.5, f32[32,640]{1,0:T(8,128)S(1)} %get-tuple-element.9.wide_ref, f32[16,128]{1,0:T(8,128)S(1)} %get-tuple-element.10.map_ref), custom_call_target="tpu_custom_call" | custom-call | flops 2013265920 | bytes 6905856 | tf_op jit(solution)/shard_map/pallas_call | solution.py:151
  (2 shorter events, 0.0 us)
Async XLA Ops:
  7.2 47.7 %copy-start.1 = (bf16[768,640]{1,0:T(8,128)(2,1)S(1)}, bf16[768,640]{1,0:T(8,128)(2,1)}, u32[]{:S(2)}) copy-start(bf16[768,640]{1,0:T(8,128)(2,1)} %acts_ref.5) | copy-start | bytes 2949124
  7.2 91.0 %all-gather.2.cloned.1.call-start = ((), (), s32[]{:S(2)}) async-start(), calls=%async_computation.7 | async-start | bytes 3538944 | tf_op jit(solution)/shard_map/all_gather | solution.py:174
  7.9 1.0 copy-start.2
  8.9 0.8 copy-start.4
  28.2 1.2 %copy-start = (bf16[768,640]{1,0:T(8,128)(2,1)S(1)}, bf16[768,640]{1,0:T(8,128)(2,1)}, u32[]{:S(2)}) copy-start(bf16[768,640]{1,0:T(8,128)(2,1)} %acts_ref.5) | copy-start | bytes 2949124
  29.4 38.8 %copy-start.3 = (bf16[768,256]{1,0:T(8,128)(2,1)S(1)}, bf16[768,256]{1,0:T(8,128)(2,1)}, u32[]{:S(2)}) copy-start(bf16[768,256]{1,0:T(8,128)(2,1)} %grads_ref.3) | copy-start | bytes 1179652
  88.0 10.1 %all-to-all-start.6 = ((f32[8,4,256]{2,1,0:T(4,128)}), f32[8,4,256]{2,1,0:T(4,128)S(1)}, u32[]{:S(2)}, u32[]{:S(2)}) async-start(f32[8,4,256]{2,1,0:T(4,128)} %shard_map.65), calls=%async_computation.6 | async-start | bytes 65536 | tf_op jit(solution)/shard_map/all_to_all | solution.py:162
  98.1 1.9 %copy-start.5 = (bf16[768,2048]{1,0:T(8,128)(2,1)S(1)}, bf16[768,2048]{1,0:T(8,128)(2,1)}, u32[]{:S(2)}) copy-start(bf16[768,2048]{1,0:T(8,128)(2,1)} %all-gather.2.cloned.1.call-done.grads_ref) | copy-start | bytes 9437188
Sparse Core Ops, SparseCore 0:
  10.0 64.7 all-gather.1

commit v3 on v2

--- a/solution.py
+++ b/solution.py
@@ -117,31 +117,43 @@
             wide_ref[rank * i + k:rank * i + k + 1, :] = split[a]
 
 
+def gradient_kernel(acts_ref, grads_ref, out_ref):
+    width = grads_ref.shape[2]
+    for i in range(grads_ref.shape[0]):
+        out_ref[:, i * width:(i + 1) * width] = lax.dot_general(
+            acts_ref[...], grads_ref[i], (((0,), (0,)), ((), ())), preferred_element_type=F32
+        )
+
+
 def residual_kernel(
-    scale, parts_ref, acts_ref, grads_ref, wide_ref, map_ref, factor_ref, out_ref, held
+    scale, tile, parts_ref, whole_ref, wide_ref, map_ref, factor_ref, out_ref, held, rounded, sems
 ):
     ways, rank, _ = parts_ref.shape
-
-    @pl.when(pl.program_id(0) == 0)
-    def _():
-        y = jnp.concatenate([parts_ref[i] for i in range(ways)], axis=1) * scale
-        held[...] = jnp.zeros_like(held)
-        for k in range(rank):
-            line = functools.reduce(
-                jnp.add,
-                [map_ref[rank * k + j:rank * k + j + 1, 0:1] * y[j:j + 1] for j in range(rank)],
-            )
-            factor_ref[k:k + 1, :] = line
-            split = pieces(line)
-            for i, (_, b) in enumerate(PIECE_PAIRS):
-                held[rank * i + k:rank * i + k + 1, :] = split[b]
-
-    first = (((0,), (0,)), ((), ()))
-    whole = lax.dot_general(acts_ref[...], grads_ref[...], first, preferred_element_type=F32)
-    approx = lax.dot_general(
-        wide_ref[...].astype(BF16), held[...].astype(BF16), first, preferred_element_type=F32
-    )
-    out_ref[0] = (whole - approx).astype(out_ref.dtype)
+    y = jnp.concatenate([parts_ref[i] for i in range(ways)], axis=1) * scale
+    held[...] = jnp.zeros_like(held)
+    for k in range(rank):
+        line = functools.reduce(
+            jnp.add,
+            [map_ref[rank * k + j:rank * k + j + 1, 0:1] * y[j:j + 1] for j in range(rank)],
+        )
+        factor_ref[k:k + 1, :] = line
+        split = pieces(line)
+        for i, (_, b) in enumerate(PIECE_PAIRS):
+            held[rank * i + k:rank * i + k + 1, :] = split[b]
+    rows = held[...].astype(BF16)
+    copies = []
+    for i in range(whole_ref.shape[0] // tile):
+        span = slice(i * tile, (i + 1) * tile)
+        approx = lax.dot_general(
+            wide_ref[:, span].astype(BF16), rows, (((0,), (0,)), ((), ())),
+            preferred_element_type=F32,
+        )
+        rounded[span] = (whole_ref[span] - approx).astype(rounded.dtype)
+        place = pl.ds(i * tile, tile)
+        copies.append(pltpu.make_async_copy(rounded.at[place], out_ref.at[0, place], sems.at[i]))
+        copies[-1].start()
+    for copy in copies:
+        copy.wait()
 
 
 def call(kernel, outs, args, scratch, flops, grid=None):
@@ -171,7 +183,10 @@
     rows = lambda n: pltpu.VMEM((16, n), F32)
     shape = lambda *dims: jax.ShapeDtypeStruct(dims, F32)
 
-    grads = lax.all_gather(out_grads, "mp", axis=1, tiled=True)
+    grads = lax.all_gather(out_grads, "mp", axis=0)
+    hbm = pl.BlockSpec(memory_space=pltpu.HBM)
+    vmem = pl.BlockSpec(memory_space=pltpu.VMEM)
+    sems = pltpu.SemaphoreType.DMA
 
     coeffs = call(
         coeff_kernel, [shape(ways, rank, tokens)], [prev_factor, out_grads],
@@ -202,24 +217,25 @@
     right = exchange(right, "mp")
 
     tile = 128
-    whole = lambda *dims: pl.BlockSpec(dims, lambda i: (0,) * len(dims))
-    factor, residual = call(
-        functools.partial(residual_kernel, 1.0 / replicas),
-        [shape(rank, width), jax.ShapeDtypeStruct((1, units, width), BF16)],
-        [right, hidden_acts, grads, wide, maps],
-        [pltpu.VMEM((32, width), F32)],
+    gradient = call(
+        gradient_kernel, [shape(units, width)], [hidden_acts, grads], [],
         2 * tokens * units * width,
         dict(
             grid=(units // tile,),
             in_specs=[
-                whole(ways, rank, part),
                 pl.BlockSpec((tokens, tile), lambda i: (0, i)),
-                whole(tokens, width),
-                pl.BlockSpec((32, tile), lambda i: (0, i)),
-                whole(rank * rank, 128),
+                pl.BlockSpec((ways, tokens, part), lambda i: (0, 0, 0)),
             ],
-            out_specs=[whole(rank, width), pl.BlockSpec((1, tile, width), lambda i: (0, i, 0))],
+            out_specs=pl.BlockSpec((tile, width), lambda i: (i, 0)),
         ),
+    )
+    factor, residual = call(
+        functools.partial(residual_kernel, 1.0 / replicas, tile),
+        [shape(rank, width), jax.ShapeDtypeStruct((1, units, width), BF16)],
+        [right, gradient, wide, maps],
+        [pltpu.VMEM((32, width), F32), pltpu.VMEM((units, width), BF16), sems((units // tile,))],
+        64 * units * width,
+        dict(in_specs=[vmem] * 4, out_specs=[vmem, hbm]),
     )
     return basis, factor, residual
 

time: 113 us -> 114 us (level)
  blocking collectives: 75.3 us -> 66.9 us
  local copies, waits for them, and re-layouts: 4.85 us -> 9.62 us
  starting transfers between devices: 3.38 us -> 6.72 us
  Pallas kernels: 8.14 us -> 9.64 us
    all_to_all x6 -> x5, blocking collectives: 75.3 us -> 66.9 us  [exchange(): return lax.all_to_all(copies, axis, 0, 0, tiled=True)]
    unnamed x12 -> x16, local copies, waits for them, and re-layouts: 4.85 us -> 9.62 us
    all_to_all x1 -> x2, starting transfers between devices: 3.34 us -> 6.68 us  [exchange(): return lax.all_to_all(copies, axis, 0, 0, tiled=True)]
    pallas_call x9 -> x10, Pallas kernels: 8.14 us -> 9.64 us  [call(): pl.pallas_call(kernel, out_shape=outs[0] if single else outs, scratch_sha...]
    all_to_all x1 -> x2, waiting for transfers between devices: 5.5 us -> 5.6 us  [exchange(): return lax.all_to_all(copies, axis, 0, 0, tiled=True)]
  transfers between devices with their start and end apart: 2 -> 3, of which waited for: 1 -> 1; matrix products, arithmetic and copies ran while one was open for 0% -> 0% of each run, Pallas kernels for 3% -> 6%
where the time goes in v3:
time: 114 us; the launch traced here: 113 us
  blocking collectives  66.9 us (59%)
  between operations  14.1 us (12%)
  Pallas kernels  9.64 us (8%)
  local copies, waits for them, and re-layouts  9.62 us (8%)
  starting transfers between devices  6.72 us (6%)
  waiting for transfers between devices  6.31 us (6%)
    all_to_all x5, blocking collectives, exchange(): return lax.all_to_all(copies, axis, 0, 0, tiled=True)  66.9 us
    pallas_call x10, Pallas kernels, call(): pl.pallas_call(kernel, out_shape=outs[0] if single else outs, scratch_sha...  9.64 us
    unnamed x16, local copies, waits for them, and re-layouts  9.62 us
    all_to_all x2, starting transfers between devices, exchange(): return lax.all_to_all(copies, axis, 0, 0, tiled=True)  6.68 us
    all_to_all x2, waiting for transfers between devices, exchange(): return lax.all_to_all(copies, axis, 0, 0, tiled=True)  5.6 us
  transfers between devices with their start and end apart: 3, of which 1 were waited for; matrix products, arithmetic and copies ran while one was open for 0% of the time, Pallas kernels for 6%

profile of v3, /device:TPU:1, one launch (start us, length us, event | category | flops | bytes accessed | tf_op | source)
XLA Modules:
  0.0 113.3 jit_solution(6608780215366149958)
XLA Ops:
  7.2 0.0 copy-start.3
  7.2 0.0 all-gather.3.cloned.1.call-start
  7.2 0.7 all-gather.3.cloned.1.call-update
  7.9 0.0 copy-start.4
  7.9 1.0 copy-done.4
  8.9 0.0 copy-start.7
  8.9 0.8 copy-done.7
  9.7 0.3 shard_map.58
  9.9 18.3 %all_to_all.35.parts_ref = f32[8,4,768]{2,1,0:T(4,128)S(1)} all-to-all(f32[8,4,768]{2,1,0:T(4,128)S(1)} %shard_map.58), channel_id=1, replica_groups=mesh['far'=8,'near'=8,'mp'=8] {'mp'}, dimensions={0} | all-to-all | bytes 196608 | tf_op jit(solution)/shard_map/all_to_all | solution.py:174
  28.2 0.0 copy-start.2
  28.2 1.2 %copy-done.2 = bf16[768,640]{1,0:T(8,128)(2,1)S(1)} copy-done((bf16[768,640]{1,0:T(8,128)(2,1)S(1)}, bf16[768,640]{1,0:T(8,128)(2,1)}, u32[]{:S(2)}) %copy-start.2) | copy-done | bytes 983064
  29.4 0.0 copy-start.5
  29.4 0.3 shard_map.59
  29.7 11.1 %all_to_all.36.parts_ref = f32[8,4,640]{2,1,0:T(4,128)S(1)} all-to-all(f32[8,4,640]{2,1,0:T(4,128)S(1)} %shard_map.59), channel_id=1, replica_groups=mesh['far'=8,'near'=8,'mp'=8] {'near'}, dimensions={0} | all-to-all | bytes 163840 | tf_op jit(solution)/shard_map/all_to_all | solution.py:174
  40.8 14.1 %all_to_all.37.parts_ref = f32[8,4,640]{2,1,0:T(4,128)S(1)} all-to-all(f32[8,4,640]{2,1,0:T(4,128)S(1)} %shard_map.60), channel_id=1, replica_groups=mesh['far'=8,'near'=8,'mp'=8] {'far'}, dimensions={0} | all-to-all | bytes 163840 | tf_op jit(solution)/shard_map/all_to_all | solution.py:174
  54.9 0.0 copy-done.3
  54.9 0.4 shard_map.61
  55.3 13.0 %all_to_all.38.parts_ref = f32[8,4,1408]{2,1,0:T(4,128)S(1)} all-to-all(f32[8,4,1408]{2,1,0:T(4,128)S(1)} %shard_map.61), channel_id=1, replica_groups=mesh['far'=8,'near'=8,'mp'=8] {'mp'}, dimensions={0} | all-to-all | bytes 360448 | tf_op jit(solution)/shard_map/all_to_all | solution.py:174
  68.3 0.0 copy-done.5
  68.3 0.2 shard_map.63
  68.5 10.3 %all_to_all.39.parts_ref = f32[8,4,256]{2,1,0:T(4,128)S(1)} all-to-all(f32[8,4,256]{2,1,0:T(4,128)S(1)} %shard_map.63), channel_id=1, replica_groups=mesh['far'=8,'near'=8,'mp'=8] {'near'}, dimensions={0} | all-to-all | bytes 65536 | tf_op jit(solution)/shard_map/all_to_all | solution.py:174
  78.9 0.6 shard_map.64
  79.5 3.3 %all-to-all-start.5 = ((f32[8,4,256]{2,1,0:T(4,128)}), f32[8,4,256]{2,1,0:T(4,128)S(1)}, u32[]{:S(2)}, u32[]{:S(2)}) async-start(f32[8,4,256]{2,1,0:T(4,128)} %shard_map.64), calls=%async_computation.5 | async-start | bytes 65536 | tf_op jit(solution)/shard_map/all_to_all | solution.py:174
  82.8 1.3 %shard_map.62 = (f32[4,640]{1,0:T(4,128)}, f32[32,640]{1,0:T(8,128)S(1)}, f32[16,128]{1,0:T(8,128)S(1)}) custom-call(f32[8,4,1408]{2,1,0:T(4,128)S(1)} %all_to_all.38.parts_ref), custom_call_target="tpu_custom_call" | custom-call | flops 512000 | bytes 280576 | tf_op jit(solution)/shard_map/pallas_call | solution.py:163
  84.1 5.6 %all-to-all-done.5.parts_ref = f32[8,4,256]{2,1,0:T(4,128)S(1)} async-done(((f32[8,4,256]{2,1,0:T(4,128)}), f32[8,4,256]{2,1,0:T(4,128)S(1)}, u32[]{:S(2)}, u32[]{:S(2)}) %all-to-all-start.5) | async-done | bytes 32800 | tf_op jit(solution)/shard_map/all_to_all | solution.py:174
  89.7 0.6 shard_map.65
  90.4 3.3 %all-to-all-start.6 = ((f32[8,4,256]{2,1,0:T(4,128)}), f32[8,4,256]{2,1,0:T(4,128)S(1)}, u32[]{:S(2)}, u32[]{:S(2)}) async-start(f32[8,4,256]{2,1,0:T(4,128)} %shard_map.65), calls=%async_computation.6 | async-start | bytes 65536 | tf_op jit(solution)/shard_map/all_to_all | solution.py:174
  93.7 0.0 all-gather.3.cloned.1.call-done
  93.7 0.0 copy-start.6
  93.7 1.9 %copy-done.6 = bf16[6144,256]{1,0:T(8,128)(2,1)S(1)} copy-done((bf16[6144,256]{1,0:T(8,128)(2,1)S(1)}, bf16[6144,256]{1,0:T(8,128)(2,1)}, u32[]{:S(2)}) %copy-start.6) | copy-done | bytes 3145752
  95.6 3.4 %shard_map.66.whole_ref = f32[640,2048]{1,0:T(8,128)S(1)} custom-call(bf16[768,640]{1,0:T(8,128)(2,1)S(1)} %copy-done.3, bf16[8,768,256]{2,1,0:T(8,128)(2,1)S(1)} %bitcast.1), custom_call_target="tpu_custom_call" | custom-call | flops 2013265920 | bytes 9371648 | tf_op jit(solution)/shard_map/pallas_call | solution.py:163
  99.0 0.0 copy-start
  99.0 2.3 %copy-done = f32[640,2048]{1,0:T(8,128)} copy-done((f32[640,2048]{1,0:T(8,128)}, f32[640,2048]{1,0:T(8,128)S(1)}, u32[]{:S(2)}) %copy-start) | copy-done | bytes 5242904
  101.3 0.0 all-to-all-done.6.parts_ref
  101.3 0.0 copy-start.1
  101.3 2.5 %copy-done.1 = f32[640,2048]{1,0:T(8,128)S(1)} copy-done((f32[640,2048]{1,0:T(8,128)S(1)}, f32[640,2048]{1,0:T(8,128)}, u32[]{:S(2)}) %copy-start.1) | copy-done | bytes 5242904
  103.8 2.6 %shard_map.67 = (f32[4,2048]{1,0:T(4,128)}, bf16[1,640,2048]{2,1,0:T(8,128)(2,1)}) custom-call(f32[8,4,256]{2,1,0:T(4,128)S(1)} %all-to-all-done.6.parts_ref, f32[640,2048]{1,0:T(8,128)S(1)} %copy-done.1, f32[32,640]{1,0:T(8,128)S(1)} %get-tuple-element.9.wide_ref, f32[16,128]{1,0:T(8,128)S(1)} %get-tuple-element.10.map_ref), custom_call_target="tpu_custom_call" | custom-call | flops 83886080 | bytes 8019968 | tf_op jit(solution)/shard_map/pallas_call | solution.py:163
  (1 shorter events, 0.0 us)
Async XLA Ops:
  7.2 47.8 %copy-start.3 = (bf16[768,640]{1,0:T(8,128)(2,1)S(1)}, bf16[768,640]{1,0:T(8,128)(2,1)}, u32[]{:S(2)}) copy-start(bf16[768,640]{1,0:T(8,128)(2,1)} %acts_ref.5) | copy-start | bytes 2949124
  7.2 86.6 %all-gather.3.cloned.1.call-start = ((), (), s32[]{:S(2)}) async-start(), calls=%async_computation.7 | async-start | bytes 3538944 | tf_op jit(solution)/shard_map/all_gather | solution.py:186
  7.9 1.0 copy-start.4
  8.9 0.8 copy-start.7
  28.2 1.2 %copy-start.2 = (bf16[768,640]{1,0:T(8,128)(2,1)S(1)}, bf16[768,640]{1,0:T(8,128)(2,1)}, u32[]{:S(2)}) copy-start(bf16[768,640]{1,0:T(8,128)(2,1)} %acts_ref.5) | copy-start | bytes 2949124
  29.4 38.9 %copy-start.5 = (bf16[768,256]{1,0:T(8,128)(2,1)S(1)}, bf16[768,256]{1,0:T(8,128)(2,1)}, u32[]{:S(2)}) copy-start(bf16[768,256]{1,0:T(8,128)(2,1)} %grads_ref.3) | copy-start | bytes 1179652
  79.5 10.2 %all-to-all-start.5 = ((f32[8,4,256]{2,1,0:T(4,128)}), f32[8,4,256]{2,1,0:T(4,128)S(1)}, u32[]{:S(2)}, u32[]{:S(2)}) async-start(f32[8,4,256]{2,1,0:T(4,128)} %shard_map.64), calls=%async_computation.5 | async-start | bytes 65536 | tf_op jit(solution)/shard_map/all_to_all | solution.py:174
  90.4 10.9 %all-to-all-start.6 = ((f32[8,4,256]{2,1,0:T(4,128)}), f32[8,4,256]{2,1,0:T(4,128)S(1)}, u32[]{:S(2)}, u32[]{:S(2)}) async-start(f32[8,4,256]{2,1,0:T(4,128)} %shard_map.65), calls=%async_computation.6 | async-start | bytes 65536 | tf_op jit(solution)/shard_map/all_to_all | solution.py:174
  93.7 1.9 %copy-start.6 = (bf16[6144,256]{1,0:T(8,128)(2,1)S(1)}, bf16[6144,256]{1,0:T(8,128)(2,1)}, u32[]{:S(2)}) copy-start(bf16[6144,256]{1,0:T(8,128)(2,1)} %all-gather.3.cloned.1.call-done) | copy-start | bytes 9437188
  99.0 2.3 %copy-start = (f32[640,2048]{1,0:T(8,128)}, f32[640,2048]{1,0:T(8,128)S(1)}, u32[]{:S(2)}) copy-start(f32[640,2048]{1,0:T(8,128)S(1)} %shard_map.66.whole_ref) | copy-start | bytes 15728644
  101.3 2.5 %copy-start.1 = (f32[640,2048]{1,0:T(8,128)S(1)}, f32[640,2048]{1,0:T(8,128)}, u32[]{:S(2)}) copy-start(f32[640,2048]{1,0:T(8,128)} %copy-done) | copy-start | bytes 15728644
Sparse Core Ops, SparseCore 0:
  10.1 55.6 all-gather.2

commit v4 on v2

--- a/solution.py
+++ b/solution.py
@@ -118,30 +118,38 @@
 
 
 def residual_kernel(
-    scale, parts_ref, acts_ref, grads_ref, wide_ref, map_ref, factor_ref, out_ref, held
+    scale, parts_ref, acts_ref, grads_ref, wide_ref, map_ref, factor_ref, out_ref,
+    turned, held, rounded, sems,
 ):
-    ways, rank, _ = parts_ref.shape
-
-    @pl.when(pl.program_id(0) == 0)
-    def _():
-        y = jnp.concatenate([parts_ref[i] for i in range(ways)], axis=1) * scale
+    ways, rank, width = parts_ref.shape
+    turned[...] = acts_ref[...].T
+    left = wide_ref[...].astype(BF16)
+    maps = [map_ref[i:i + 1, 0:1] for i in range(rank * rank)]
+    copies = []
+    for i in range(ways):
+        span = slice(i * width, (i + 1) * width)
+        y = parts_ref[i] * scale
         held[...] = jnp.zeros_like(held)
         for k in range(rank):
             line = functools.reduce(
-                jnp.add,
-                [map_ref[rank * k + j:rank * k + j + 1, 0:1] * y[j:j + 1] for j in range(rank)],
+                jnp.add, [maps[rank * k + j] * y[j:j + 1] for j in range(rank)]
             )
-            factor_ref[k:k + 1, :] = line
+            factor_ref[k:k + 1, span] = line
             split = pieces(line)
-            for i, (_, b) in enumerate(PIECE_PAIRS):
-                held[rank * i + k:rank * i + k + 1, :] = split[b]
-
-    first = (((0,), (0,)), ((), ()))
-    whole = lax.dot_general(acts_ref[...], grads_ref[...], first, preferred_element_type=F32)
-    approx = lax.dot_general(
-        wide_ref[...].astype(BF16), held[...].astype(BF16), first, preferred_element_type=F32
-    )
-    out_ref[0] = (whole - approx).astype(out_ref.dtype)
+            for n, (_, b) in enumerate(PIECE_PAIRS):
+                held[rank * n + k:rank * n + k + 1, :] = -split[b]
+        whole = jnp.dot(turned[...], grads_ref[i], preferred_element_type=F32)
+        less = lax.dot_general(
+            left, held[...].astype(BF16), (((0,), (0,)), ((), ())), preferred_element_type=F32
+        )
+        rounded[:, span] = (whole + less).astype(rounded.dtype)
+        place = pl.ds(i * width, width)
+        copies.append(
+            pltpu.make_async_copy(rounded.at[:, place], out_ref.at[0, :, place], sems.at[i])
+        )
+        copies[-1].start()
+    for copy in copies:
+        copy.wait()
 
 
 def call(kernel, outs, args, scratch, flops, grid=None):
@@ -171,7 +179,10 @@
     rows = lambda n: pltpu.VMEM((16, n), F32)
     shape = lambda *dims: jax.ShapeDtypeStruct(dims, F32)
 
-    grads = lax.all_gather(out_grads, "mp", axis=1, tiled=True)
+    grads = lax.all_gather(out_grads, "mp", axis=0)
+    hbm = pl.BlockSpec(memory_space=pltpu.HBM)
+    vmem = pl.BlockSpec(memory_space=pltpu.VMEM)
+    sems = pltpu.SemaphoreType.DMA
 
     coeffs = call(
         coeff_kernel, [shape(ways, rank, tokens)], [prev_factor, out_grads],
@@ -201,25 +212,16 @@
     right = call(sum_kernel, [shape(ways, rank, part)], [exchange(right, "far")], [], 8 * part)
     right = exchange(right, "mp")
 
-    tile = 128
-    whole = lambda *dims: pl.BlockSpec(dims, lambda i: (0,) * len(dims))
     factor, residual = call(
         functools.partial(residual_kernel, 1.0 / replicas),
         [shape(rank, width), jax.ShapeDtypeStruct((1, units, width), BF16)],
         [right, hidden_acts, grads, wide, maps],
-        [pltpu.VMEM((32, width), F32)],
+        [
+            pltpu.VMEM((units, tokens), BF16), pltpu.VMEM((32, part), F32),
+            pltpu.VMEM((units, width), BF16), sems((ways,)),
+        ],
         2 * tokens * units * width,
-        dict(
-            grid=(units // tile,),
-            in_specs=[
-                whole(ways, rank, part),
-                pl.BlockSpec((tokens, tile), lambda i: (0, i)),
-                whole(tokens, width),
-                pl.BlockSpec((32, tile), lambda i: (0, i)),
-                whole(rank * rank, 128),
-            ],
-            out_specs=[whole(rank, width), pl.BlockSpec((1, tile, width), lambda i: (0, i, 0))],
-        ),
+        dict(in_specs=[vmem] * 5, out_specs=[vmem, hbm]),
     )
     return basis, factor, residual
 

time: 113 us -> 113 us (level)
  no operation moved by 1% of the time
where the time goes in v4:
time: 113 us; the launch traced here: 112 us
  blocking collectives  76.1 us (67%)
  between operations  14.1 us (12%)
  Pallas kernels  7.7 us (7%)
  waiting for transfers between devices  6.18 us (5%)
  local copies, waits for them, and re-layouts  4.85 us (4%)
  starting transfers between devices  3.38 us (3%)
    all_to_all x6, blocking collectives, exchange(): return lax.all_to_all(copies, axis, 0, 0, tiled=True)  76.1 us
    pallas_call x9, Pallas kernels, call(): pl.pallas_call(kernel, out_shape=outs[0] if single else outs, scratch_sha...  7.7 us
    all_to_all x1, waiting for transfers between devices, exchange(): return lax.all_to_all(copies, axis, 0, 0, tiled=True)  5.5 us
    unnamed x12, local copies, waits for them, and re-layouts  4.85 us
    all_to_all x1, starting transfers between devices, exchange(): return lax.all_to_all(copies, axis, 0, 0, tiled=True)  3.34 us
  transfers between devices with their start and end apart: 2, of which 1 were waited for; matrix products, arithmetic and copies ran while one was open for 0% of the time, Pallas kernels for 3%

profile of v4, /device:TPU:1, one launch (start us, length us, event | category | flops | bytes accessed | tf_op | source)
XLA Modules:
  0.0 112.3 jit_solution(15875181794540684046)
XLA Ops:
  7.2 0.0 copy-start.1
  7.2 0.0 all-gather.3.cloned.1.call-start
  7.2 0.7 all-gather.3.cloned.1.call-update
  7.9 0.0 copy-start.2
  7.9 1.0 copy-done.2
  8.9 0.0 copy-start.4
  8.9 0.8 copy-done.4
  9.7 0.3 shard_map.58
  9.9 18.3 %all_to_all.35.parts_ref = f32[8,4,768]{2,1,0:T(4,128)S(1)} all-to-all(f32[8,4,768]{2,1,0:T(4,128)S(1)} %shard_map.58), channel_id=1, replica_groups=mesh['far'=8,'near'=8,'mp'=8] {'mp'}, dimensions={0} | all-to-all | bytes 196608 | tf_op jit(solution)/shard_map/all_to_all | solution.py:170
  28.2 0.0 copy-start
  28.2 1.2 %copy-done = bf16[768,640]{1,0:T(8,128)(2,1)S(1)} copy-done((bf16[768,640]{1,0:T(8,128)(2,1)S(1)}, bf16[768,640]{1,0:T(8,128)(2,1)}, u32[]{:S(2)}) %copy-start) | copy-done | bytes 983064
  29.4 0.0 copy-start.3
  29.4 0.3 shard_map.59
  29.7 11.1 %all_to_all.36.parts_ref = f32[8,4,640]{2,1,0:T(4,128)S(1)} all-to-all(f32[8,4,640]{2,1,0:T(4,128)S(1)} %shard_map.59), channel_id=1, replica_groups=mesh['far'=8,'near'=8,'mp'=8] {'near'}, dimensions={0} | all-to-all | bytes 163840 | tf_op jit(solution)/shard_map/all_to_all | solution.py:170
  40.8 14.1 %all_to_all.37.parts_ref = f32[8,4,640]{2,1,0:T(4,128)S(1)} all-to-all(f32[8,4,640]{2,1,0:T(4,128)S(1)} %shard_map.60), channel_id=1, replica_groups=mesh['far'=8,'near'=8,'mp'=8] {'far'}, dimensions={0} | all-to-all | bytes 163840 | tf_op jit(solution)/shard_map/all_to_all | solution.py:170
  54.9 0.0 copy-done.1
  54.9 0.4 shard_map.61
  55.3 13.0 %all_to_all.38.parts_ref = f32[8,4,1408]{2,1,0:T(4,128)S(1)} all-to-all(f32[8,4,1408]{2,1,0:T(4,128)S(1)} %shard_map.61), channel_id=1, replica_groups=mesh['far'=8,'near'=8,'mp'=8] {'mp'}, dimensions={0} | all-to-all | bytes 360448 | tf_op jit(solution)/shard_map/all_to_all | solution.py:170
  68.3 0.0 copy-done.3
  68.3 0.2 shard_map.63
  68.5 10.3 %all_to_all.39.parts_ref = f32[8,4,256]{2,1,0:T(4,128)S(1)} all-to-all(f32[8,4,256]{2,1,0:T(4,128)S(1)} %shard_map.63), channel_id=1, replica_groups=mesh['far'=8,'near'=8,'mp'=8] {'near'}, dimensions={0} | all-to-all | bytes 65536 | tf_op jit(solution)/shard_map/all_to_all | solution.py:170
  78.9 9.2 %all_to_all.40.parts_ref = f32[8,4,256]{2,1,0:T(4,128)S(1)} all-to-all(f32[8,4,256]{2,1,0:T(4,128)S(1)} %shard_map.64), channel_id=1, replica_groups=mesh['far'=8,'near'=8,'mp'=8] {'far'}, dimensions={0} | all-to-all | bytes 65536 | tf_op jit(solution)/shard_map/all_to_all | solution.py:170
  88.1 0.6 shard_map.65
  88.7 3.3 %all-to-all-start.6 = ((f32[8,4,256]{2,1,0:T(4,128)}), f32[8,4,256]{2,1,0:T(4,128)S(1)}, u32[]{:S(2)}, u32[]{:S(2)}) async-start(f32[8,4,256]{2,1,0:T(4,128)} %shard_map.65), calls=%async_computation.6 | async-start | bytes 65536 | tf_op jit(solution)/shard_map/all_to_all | solution.py:170
  92.1 1.3 %shard_map.62 = (f32[4,640]{1,0:T(4,128)}, f32[32,640]{1,0:T(8,128)S(1)}, f32[16,128]{1,0:T(8,128)S(1)}) custom-call(f32[8,4,1408]{2,1,0:T(4,128)S(1)} %all_to_all.38.parts_ref), custom_call_target="tpu_custom_call" | custom-call | flops 512000 | bytes 280576 | tf_op jit(solution)/shard_map/pallas_call | solution.py:159
  93.4 5.5 %all-to-all-done.6.parts_ref = f32[8,4,256]{2,1,0:T(4,128)S(1)} async-done(((f32[8,4,256]{2,1,0:T(4,128)}), f32[8,4,256]{2,1,0:T(4,128)S(1)}, u32[]{:S(2)}, u32[]{:S(2)}) %all-to-all-start.6) | async-done | bytes 32800 | tf_op jit(solution)/shard_map/all_to_all | solution.py:170
  98.9 0.0 all-gather.3.cloned.1.call-done
  98.9 0.0 copy-start.5
  98.9 1.9 %copy-done.5 = bf16[6144,256]{1,0:T(8,128)(2,1)S(1)} copy-done((bf16[6144,256]{1,0:T(8,128)(2,1)S(1)}, bf16[6144,256]{1,0:T(8,128)(2,1)}, u32[]{:S(2)}) %copy-start.5) | copy-done | bytes 3145752
  100.8 4.7 %shard_map.66 = (f32[4,2048]{1,0:T(4,128)}, bf16[1,640,2048]{2,1,0:T(8,128)(2,1)}) custom-call(f32[8,4,256]{2,1,0:T(4,128)S(1)} %all-to-all-done.6.parts_ref, bf16[768,640]{1,0:T(8,128)(2,1)S(1)} %copy-done.1, bf16[8,768,256]{2,1,0:T(8,128)(2,1)S(1)} %bitcast.1, f32[32,640]{1,0:T(8,128)S(1)} %get-tuple-element.9.wide_ref, ...), custom_call_target="tpu_custom_call" | custom-call | flops 2013265920 | bytes 6905856 | tf_op jit(solution)/shard_map/pallas_call | solution.py:159
  (2 shorter events, 0.0 us)
Async XLA Ops:
  7.2 47.8 %copy-start.1 = (bf16[768,640]{1,0:T(8,128)(2,1)S(1)}, bf16[768,640]{1,0:T(8,128)(2,1)}, u32[]{:S(2)}) copy-start(bf16[768,640]{1,0:T(8,128)(2,1)} %acts_ref.5) | copy-start | bytes 2949124
  7.2 91.7 %all-gather.3.cloned.1.call-start = ((), (), s32[]{:S(2)}) async-start(), calls=%async_computation.7 | async-start | bytes 3538944 | tf_op jit(solution)/shard_map/all_gather | solution.py:182
  7.9 1.0 copy-start.2
  8.9 0.8 copy-start.4
  28.2 1.2 %copy-start = (bf16[768,640]{1,0:T(8,128)(2,1)S(1)}, bf16[768,640]{1,0:T(8,128)(2,1)}, u32[]{:S(2)}) copy-start(bf16[768,640]{1,0:T(8,128)(2,1)} %acts_ref.5) | copy-start | bytes 2949124
  29.4 38.9 %copy-start.3 = (bf16[768,256]{1,0:T(8,128)(2,1)S(1)}, bf16[768,256]{1,0:T(8,128)(2,1)}, u32[]{:S(2)}) copy-start(bf16[768,256]{1,0:T(8,128)(2,1)} %grads_ref.3) | copy-start | bytes 1179652
  88.7 10.1 %all-to-all-start.6 = ((f32[8,4,256]{2,1,0:T(4,128)}), f32[8,4,256]{2,1,0:T(4,128)S(1)}, u32[]{:S(2)}, u32[]{:S(2)}) async-start(f32[8,4,256]{2,1,0:T(4,128)} %shard_map.65), calls=%async_computation.6 | async-start | bytes 65536 | tf_op jit(solution)/shard_map/all_to_all | solution.py:170
  98.9 1.9 %copy-start.5 = (bf16[6144,256]{1,0:T(8,128)(2,1)S(1)}, bf16[6144,256]{1,0:T(8,128)(2,1)}, u32[]{:S(2)}) copy-start(bf16[6144,256]{1,0:T(8,128)(2,1)} %all-gather.3.cloned.1.call-done) | copy-start | bytes 9437188
Sparse Core Ops, SparseCore 0:
  10.1 55.6 all-gather.2

commit v5 on v4

--- a/solution.py
+++ b/solution.py
@@ -59,70 +59,93 @@
     spread(out_ref, jnp.sum(parts_ref[...], axis=0))
 
 
-def back_kernel(scale, parts_ref, acts_ref, out_ref, stack):
-    units = acts_ref.shape[1]
+def total(x):
+    return jnp.sum(jnp.sum(x, axis=1, keepdims=True), axis=0, keepdims=True)
+
+
+def inverse_root(square):
+    inverse = lax.rsqrt(square)
+    return inverse * (1.5 - 0.5 * (square * inverse) * inverse)
+
+
+def triangle(raw):
+    rank = raw.shape[0]
+    rows = [raw[k:k + 1] for k in range(rank)]
+    lane = lax.broadcasted_iota(jnp.int32, (1, 128), 1)
+    lines = [jnp.zeros((1, 128), F32) for _ in range(rank)]
+    for j in range(rank):
+        square = total(rows[j] * rows[j])
+        inverse = jnp.where(square > 0.0, inverse_root(square), 0.0)
+        unit = rows[j] * inverse
+        lines[j] = jnp.where(lane == j, square * inverse, lines[j])
+        for k in range(j + 1, rank):
+            weight = total(rows[k] * unit)
+            rows[k] = rows[k] - weight * unit
+            lines[k] = jnp.where(lane == j, weight, lines[k])
+    return lines
+
+
+def back_kernel(scale, parts_ref, acts_ref, raw_ref, out_ref, stack):
+    tokens = acts_ref.shape[0]
     raw = jnp.sum(parts_ref[...], axis=0) * scale
+    raw_ref[...] = raw
     rows = stack_pieces(raw, stack)
     product = lax.dot_general(
         rows, acts_ref[...], (((1,), (1,)), ((), ())), preferred_element_type=F32
     )
-    ways = out_ref.shape[0]
-    out_ref[:, :, :units] = jnp.broadcast_to(raw[None], (ways, *raw.shape))
-    result = fold(product, raw.shape[0])
-    out_ref[:, :, units:] = jnp.broadcast_to(result[None], (ways, *result.shape))
-
-
-def right_kernel(units, parts_ref, grads_ref, out_ref, stack):
-    rows = stack_pieces(jnp.sum(parts_ref[:, :, units:], axis=0), stack)
+    ways, rank, _ = out_ref.shape
+    result = fold(product, rank)
+    out_ref[:, :, :tokens] = jnp.broadcast_to(result[None], (ways, rank, tokens))
+    for k, line in enumerate(triangle(raw)):
+        out_ref[:, k:k + 1, tokens:] = jnp.broadcast_to(line[None], (ways, 1, 128))
+
+
+def right_kernel(parts_ref, grads_ref, out_ref, stack):
+    tokens = grads_ref.shape[0]
+    rows = stack_pieces(jnp.sum(parts_ref[:, :, :tokens], axis=0), stack)
     product = jnp.dot(rows, grads_ref[...], preferred_element_type=F32)
     spread(out_ref, fold(product, parts_ref.shape[1]))
 
 
-def total(x):
-    return jnp.sum(jnp.sum(x, axis=1, keepdims=True), axis=0, keepdims=True)
-
-
-def basis_kernel(units, full_units, parts_ref, basis_ref, wide_ref, map_ref, rows, unit):
+def basis_kernel(
+    full_units, parts_ref, raw_ref, acts_ref, basis_ref, wide_ref, map_ref, turned_ref, rows
+):
     ways, rank, _ = parts_ref.shape
-    me = lax.axis_index("mp")
+    tokens = acts_ref.shape[0]
     for k in range(ways):
         for r in range(rank):
-            rows[r, k:k + 1, :] = parts_ref[k, r:r + 1, :units]
-    units_done, maps = [], []
+            rows[r, k:k + 1, :] = parts_ref[k, r:r + 1, tokens:]
+    done, mine, maps = [], [], []
+    wide_ref[...] = jnp.zeros_like(wide_ref)
     for k in range(rank):
         raw = rows[k]
         vector = raw
+        own = raw_ref[k:k + 1]
         line = [jnp.full((1, 1), 1.0 if j == k else 0.0, F32) for j in range(rank)]
         if k:
-            weights = [total(u * raw) for u in units_done]
-            vector = raw - functools.reduce(
-                jnp.add, [w * u for w, u in zip(weights, units_done)]
-            )
+            weights = [total(u * raw) for u in done]
+            vector = raw - functools.reduce(jnp.add, [w * u for w, u in zip(weights, done)])
+            own = own - functools.reduce(jnp.add, [w * u for w, u in zip(weights, mine)])
             for w, earlier in zip(weights, maps):
                 line = [a - w * b for a, b in zip(line, earlier)]
-        square = total(vector * vector) + 1e-06
-        inverse = lax.rsqrt(square)
-        inverse = inverse * (1.5 - 0.5 * (square * inverse) * inverse)
-        units_done.append(vector * inverse)
+        inverse = inverse_root(total(vector * vector) + 1e-06)
+        done.append(vector * inverse)
+        mine.append(own * inverse)
         maps.append([a * inverse for a in line])
-        unit[k] = units_done[k]
         for j in range(rank):
             map_ref[rank * k + j:rank * k + j + 1, :] = jnp.broadcast_to(maps[k][j], (1, 128))
-    wide_ref[...] = jnp.zeros_like(wide_ref)
-    for k in range(rank):
-        mine = unit[k, pl.ds(me, 1), :]
-        basis_ref[k:k + 1, :] = mine * math.sqrt(full_units)
-        split = pieces(mine)
+        basis_ref[k:k + 1, :] = mine[k] * math.sqrt(full_units)
+        split = pieces(mine[k])
         for i, (a, _) in enumerate(PIECE_PAIRS):
             wide_ref[rank * i + k:rank * i + k + 1, :] = split[a]
+    turned_ref[...] = acts_ref[...].T
 
 
 def residual_kernel(
-    scale, parts_ref, acts_ref, grads_ref, wide_ref, map_ref, factor_ref, out_ref,
-    turned, held, rounded, sems,
+    scale, parts_ref, turned_ref, grads_ref, wide_ref, map_ref, factor_ref, out_ref,
+    held, rounded, sems,
 ):
     ways, rank, width = parts_ref.shape
-    turned[...] = acts_ref[...].T
     left = wide_ref[...].astype(BF16)
     maps = [map_ref[i:i + 1, 0:1] for i in range(rank * rank)]
     copies = []
@@ -138,7 +161,7 @@
             split = pieces(line)
             for n, (_, b) in enumerate(PIECE_PAIRS):
                 held[rank * n + k:rank * n + k + 1, :] = -split[b]
-        whole = jnp.dot(turned[...], grads_ref[i], preferred_element_type=F32)
+        whole = jnp.dot(turned_ref[...], grads_ref[i], preferred_element_type=F32)
         less = lax.dot_general(
             left, held[...].astype(BF16), (((0,), (0,)), ((), ())), preferred_element_type=F32
         )
@@ -193,20 +216,23 @@
         [rows(tokens)], 32 * tokens * units,
     )
     left = call(sum_kernel, [shape(far, rank, units)], [exchange(left, "near")], [], 8 * units)
-    packed = call(
-        functools.partial(back_kernel, 1.0 / replicas), [shape(ways, rank, units + tokens)],
+    raw, packed = call(
+        functools.partial(back_kernel, 1.0 / replicas),
+        [shape(rank, units), shape(ways, rank, tokens + 128)],
         [exchange(left, "far"), hidden_acts], [rows(units)], 32 * tokens * units,
     )
     packed = exchange(packed, "mp")
     right = call(
-        functools.partial(right_kernel, units), [shape(near, rank, part)],
-        [packed, out_grads], [rows(tokens)], 32 * tokens * part,
-    )
-    basis, wide, maps = call(
-        functools.partial(basis_kernel, units, units * ways),
-        [shape(rank, units), shape(32, units), shape(rank * rank, 128)], [packed],
-        [pltpu.VMEM((rank, ways, units), F32), pltpu.VMEM((rank, ways, units), F32)],
-        100 * ways * units,
+        right_kernel, [shape(near, rank, part)], [packed, out_grads],
+        [rows(tokens)], 32 * tokens * part,
+    )
+    basis, wide, maps, turned = call(
+        functools.partial(basis_kernel, units * ways),
+        [
+            shape(rank, units), shape(32, units), shape(rank * rank, 128),
+            jax.ShapeDtypeStruct((units, tokens), BF16),
+        ],
+        [packed, raw, hidden_acts], [pltpu.VMEM((rank, ways, 128), F32)], 100 * ways * units,
     )
     right = call(sum_kernel, [shape(far, rank, part)], [exchange(right, "near")], [], 8 * part)
     right = call(sum_kernel, [shape(ways, rank, part)], [exchange(right, "far")], [], 8 * part)
@@ -215,11 +241,8 @@
     factor, residual = call(
         functools.partial(residual_kernel, 1.0 / replicas),
         [shape(rank, width), jax.ShapeDtypeStruct((1, units, width), BF16)],
-        [right, hidden_acts, grads, wide, maps],
-        [
-            pltpu.VMEM((units, tokens), BF16), pltpu.VMEM((32, part), F32),
-            pltpu.VMEM((units, width), BF16), sems((ways,)),
-        ],
+        [right, turned, grads, wide, maps],
+        [pltpu.VMEM((32, part), F32), pltpu.VMEM((units, width), BF16), sems((ways,))],
         2 * tokens * units * width,
         dict(in_specs=[vmem] * 5, out_specs=[vmem, hbm]),
     )

time: 113 us -> 112 us (level)
  blocking collectives: 76.1 us -> 74.2 us
    all_to_all x6, blocking collectives: 76.1 us -> 74.2 us  [exchange(): return lax.all_to_all(copies, axis, 0, 0, tiled=True)]
where the time goes in v5:
time: 112 us; the launch traced here: 111 us
  blocking collectives  74.2 us (66%)
  between operations  14.1 us (13%)
  Pallas kernels  7.91 us (7%)
  waiting for transfers between devices  6.23 us (6%)
  local copies, waits for them, and re-layouts  4.85 us (4%)
  starting transfers between devices  3.38 us (3%)
    all_to_all x6, blocking collectives, exchange(): return lax.all_to_all(copies, axis, 0, 0, tiled=True)  74.2 us
    pallas_call x9, Pallas kernels, call(): pl.pallas_call(kernel, out_shape=outs[0] if single else outs, scratch_sha...  7.91 us
    all_to_all x1, waiting for transfers between devices, exchange(): return lax.all_to_all(copies, axis, 0, 0, tiled=True)  5.54 us
    unnamed x12, local copies, waits for them, and re-layouts  4.85 us
    all_to_all x1, starting transfers between devices, exchange(): return lax.all_to_all(copies, axis, 0, 0, tiled=True)  3.34 us
  transfers between devices with their start and end apart: 2, of which 1 were waited for; matrix products, arithmetic and copies ran while one was open for 0% of the time, Pallas kernels for 3%

profile of v5, /device:TPU:1, one launch (start us, length us, event | category | flops | bytes accessed | tf_op | source)
XLA Modules:
  0.0 110.7 jit_solution(6145185627178665451)
XLA Ops:
  7.2 0.0 copy-start.1
  7.2 0.0 all-gather.3.cloned.1.call-start
  7.2 0.7 all-gather.3.cloned.1.call-update
  7.9 0.0 copy-start.2
  7.9 1.0 copy-done.2
  8.9 0.0 copy-start.4
  8.9 0.8 copy-done.4
  9.7 0.3 shard_map.58
  9.9 18.3 %all_to_all.35.parts_ref = f32[8,4,768]{2,1,0:T(4,128)S(1)} all-to-all(f32[8,4,768]{2,1,0:T(4,128)S(1)} %shard_map.58), channel_id=1, replica_groups=mesh['far'=8,'near'=8,'mp'=8] {'mp'}, dimensions={0} | all-to-all | bytes 196608 | tf_op jit(solution)/shard_map/all_to_all | solution.py:193
  28.2 0.0 copy-start
  28.2 1.2 %copy-done = bf16[768,640]{1,0:T(8,128)(2,1)S(1)} copy-done((bf16[768,640]{1,0:T(8,128)(2,1)S(1)}, bf16[768,640]{1,0:T(8,128)(2,1)}, u32[]{:S(2)}) %copy-start) | copy-done | bytes 983064
  29.4 0.0 copy-start.3
  29.4 0.3 shard_map.59
  29.7 11.1 %all_to_all.36.parts_ref = f32[8,4,640]{2,1,0:T(4,128)S(1)} all-to-all(f32[8,4,640]{2,1,0:T(4,128)S(1)} %shard_map.59), channel_id=1, replica_groups=mesh['far'=8,'near'=8,'mp'=8] {'near'}, dimensions={0} | all-to-all | bytes 163840 | tf_op jit(solution)/shard_map/all_to_all | solution.py:193
  40.8 14.1 %all_to_all.37.parts_ref = f32[8,4,640]{2,1,0:T(4,128)S(1)} all-to-all(f32[8,4,640]{2,1,0:T(4,128)S(1)} %shard_map.60), channel_id=1, replica_groups=mesh['far'=8,'near'=8,'mp'=8] {'far'}, dimensions={0} | all-to-all | bytes 163840 | tf_op jit(solution)/shard_map/all_to_all | solution.py:193
  54.9 0.0 copy-done.1
  54.9 0.6 shard_map.61
  55.6 11.2 %all_to_all.38.parts_ref = f32[8,4,896]{2,1,0:T(4,128)S(1)} all-to-all(f32[8,4,896]{2,1,0:T(4,128)S(1)} %get-tuple-element.11), channel_id=1, replica_groups=mesh['far'=8,'near'=8,'mp'=8] {'mp'}, dimensions={0} | all-to-all | bytes 229376 | tf_op jit(solution)/shard_map/all_to_all | solution.py:193
  66.7 0.0 copy-done.3
  66.7 0.2 shard_map.63
  66.9 10.3 %all_to_all.39.parts_ref = f32[8,4,256]{2,1,0:T(4,128)S(1)} all-to-all(f32[8,4,256]{2,1,0:T(4,128)S(1)} %shard_map.63), channel_id=1, replica_groups=mesh['far'=8,'near'=8,'mp'=8] {'near'}, dimensions={0} | all-to-all | bytes 65536 | tf_op jit(solution)/shard_map/all_to_all | solution.py:193
  77.2 9.2 %all_to_all.40.parts_ref = f32[8,4,256]{2,1,0:T(4,128)S(1)} all-to-all(f32[8,4,256]{2,1,0:T(4,128)S(1)} %shard_map.64), channel_id=1, replica_groups=mesh['far'=8,'near'=8,'mp'=8] {'far'}, dimensions={0} | all-to-all | bytes 65536 | tf_op jit(solution)/shard_map/all_to_all | solution.py:193
  86.5 0.6 shard_map.65
  87.1 3.3 %all-to-all-start.6 = ((f32[8,4,256]{2,1,0:T(4,128)}), f32[8,4,256]{2,1,0:T(4,128)S(1)}, u32[]{:S(2)}, u32[]{:S(2)}) async-start(f32[8,4,256]{2,1,0:T(4,128)} %shard_map.65), calls=%async_computation.6 | async-start | bytes 65536 | tf_op jit(solution)/shard_map/all_to_all | solution.py:193
  90.4 1.3 %shard_map.62 = (f32[4,640]{1,0:T(4,128)}, f32[32,640]{1,0:T(8,128)S(1)}, f32[16,128]{1,0:T(8,128)S(1)}, bf16[640,768]{1,0:T(8,128)(2,1)S(1)}) custom-call(f32[8,4,896]{2,1,0:T(4,128)S(1)} %all_to_all.38.parts_ref, f32[4,640]{1,0:T(4,128)S(1)} %get-tuple-element.12.raw_ref, bf16[768,640]{1,0:T(8,128)(2,1)S(1)} %copy-done.1), custom_call_target="tpu_custom_call" | custom-call | flops 512000 | bytes 2191360 | tf_op jit(solution)/shard_map/pallas_call | solution.py:182
  91.7 5.5 %all-to-all-done.6.parts_ref = f32[8,4,256]{2,1,0:T(4,128)S(1)} async-done(((f32[8,4,256]{2,1,0:T(4,128)}), f32[8,4,256]{2,1,0:T(4,128)S(1)}, u32[]{:S(2)}, u32[]{:S(2)}) %all-to-all-start.6) | async-done | bytes 32800 | tf_op jit(solution)/shard_map/all_to_all | solution.py:193
  97.2 0.0 all-gather.3.cloned.1.call-done
  97.2 0.0 copy-start.5
  97.2 1.9 %copy-done.5 = bf16[6144,256]{1,0:T(8,128)(2,1)S(1)} copy-done((bf16[6144,256]{1,0:T(8,128)(2,1)S(1)}, bf16[6144,256]{1,0:T(8,128)(2,1)}, u32[]{:S(2)}) %copy-start.5) | copy-done | bytes 3145752
  99.1 4.7 %shard_map.66 = (f32[4,2048]{1,0:T(4,128)}, bf16[1,640,2048]{2,1,0:T(8,128)(2,1)}) custom-call(f32[8,4,256]{2,1,0:T(4,128)S(1)} %all-to-all-done.6.parts_ref, bf16[640,768]{1,0:T(8,128)(2,1)S(1)} %get-tuple-element.14.turned_ref, bf16[8,768,256]{2,1,0:T(8,128)(2,1)S(1)} %bitcast.1, f32[32,640]{1,0:T(8,128)S(1)} %get-tuple-element.15.wide_ref, ...), custom_call_target="tpu_custom_call" | custom-call | flops 2013265920 | bytes 6905856 | tf_op jit(solution)/shard_map/pallas_call | solution.py:182
  (2 shorter events, 0.0 us)
Async XLA Ops:
  7.2 47.8 %copy-start.1 = (bf16[768,640]{1,0:T(8,128)(2,1)S(1)}, bf16[768,640]{1,0:T(8,128)(2,1)}, u32[]{:S(2)}) copy-start(bf16[768,640]{1,0:T(8,128)(2,1)} %acts_ref.5) | copy-start | bytes 2949124
  7.2 90.1 %all-gather.3.cloned.1.call-start = ((), (), s32[]{:S(2)}) async-start(), calls=%async_computation.7 | async-start | bytes 3538944 | tf_op jit(solution)/shard_map/all_gather | solution.py:205
  7.9 1.0 copy-start.2
  8.9 0.8 copy-start.4
  28.2 1.2 %copy-start = (bf16[768,640]{1,0:T(8,128)(2,1)S(1)}, bf16[768,640]{1,0:T(8,128)(2,1)}, u32[]{:S(2)}) copy-start(bf16[768,640]{1,0:T(8,128)(2,1)} %acts_ref.5) | copy-start | bytes 2949124
  29.4 37.3 %copy-start.3 = (bf16[768,256]{1,0:T(8,128)(2,1)S(1)}, bf16[768,256]{1,0:T(8,128)(2,1)}, u32[]{:S(2)}) copy-start(bf16[768,256]{1,0:T(8,128)(2,1)} %grads_ref.3) | copy-start | bytes 1179652
  87.1 10.1 %all-to-all-start.6 = ((f32[8,4,256]{2,1,0:T(4,128)}), f32[8,4,256]{2,1,0:T(4,128)S(1)}, u32[]{:S(2)}, u32[]{:S(2)}) async-start(f32[8,4,256]{2,1,0:T(4,128)} %shard_map.65), calls=%async_computation.6 | async-start | bytes 65536 | tf_op jit(solution)/shard_map/all_to_all | solution.py:193
  97.2 1.9 %copy-start.5 = (bf16[6144,256]{1,0:T(8,128)(2,1)S(1)}, bf16[6144,256]{1,0:T(8,128)(2,1)}, u32[]{:S(2)}) copy-start(bf16[6144,256]{1,0:T(8,128)(2,1)} %all-gather.3.cloned.1.call-done) | copy-start | bytes 9437188
Sparse Core Ops, SparseCore 0:
  10.1 54.9 all-gather.2

commit v6 on v5

--- a/solution.py
+++ b/solution.py
@@ -146,24 +146,25 @@
     held, rounded, sems,
 ):
     ways, rank, width = parts_ref.shape
+    y = jnp.concatenate([parts_ref[i] for i in range(ways)], axis=1) * scale
+    held[...] = jnp.zeros_like(held)
+    for k in range(rank):
+        line = functools.reduce(
+            jnp.add,
+            [map_ref[rank * k + j:rank * k + j + 1, 0:1] * y[j:j + 1] for j in range(rank)],
+        )
+        factor_ref[k:k + 1, :] = line
+        split = pieces(line)
+        for n, (_, b) in enumerate(PIECE_PAIRS):
+            held[rank * n + k:rank * n + k + 1, :] = -split[b]
     left = wide_ref[...].astype(BF16)
-    maps = [map_ref[i:i + 1, 0:1] for i in range(rank * rank)]
+    right = held[...].astype(BF16)
     copies = []
     for i in range(ways):
         span = slice(i * width, (i + 1) * width)
-        y = parts_ref[i] * scale
-        held[...] = jnp.zeros_like(held)
-        for k in range(rank):
-            line = functools.reduce(
-                jnp.add, [maps[rank * k + j] * y[j:j + 1] for j in range(rank)]
-            )
-            factor_ref[k:k + 1, span] = line
-            split = pieces(line)
-            for n, (_, b) in enumerate(PIECE_PAIRS):
-                held[rank * n + k:rank * n + k + 1, :] = -split[b]
         whole = jnp.dot(turned_ref[...], grads_ref[i], preferred_element_type=F32)
         less = lax.dot_general(
-            left, held[...].astype(BF16), (((0,), (0,)), ((), ())), preferred_element_type=F32
+            left, right[:, span], (((0,), (0,)), ((), ())), preferred_element_type=F32
         )
         rounded[:, span] = (whole + less).astype(rounded.dtype)
         place = pl.ds(i * width, width)
@@ -235,14 +236,15 @@
         [packed, raw, hidden_acts], [pltpu.VMEM((rank, ways, 128), F32)], 100 * ways * units,
     )
     right = call(sum_kernel, [shape(far, rank, part)], [exchange(right, "near")], [], 8 * part)
-    right = call(sum_kernel, [shape(ways, rank, part)], [exchange(right, "far")], [], 8 * part)
+    right, grads = lax.optimization_barrier((exchange(right, "far"), grads))
+    right = call(sum_kernel, [shape(ways, rank, part)], [right], [], 8 * part)
     right = exchange(right, "mp")
 
     factor, residual = call(
         functools.partial(residual_kernel, 1.0 / replicas),
         [shape(rank, width), jax.ShapeDtypeStruct((1, units, width), BF16)],
         [right, turned, grads, wide, maps],
-        [pltpu.VMEM((32, part), F32), pltpu.VMEM((units, width), BF16), sems((ways,))],
+        [pltpu.VMEM((32, width), F32), pltpu.VMEM((units, width), BF16), sems((ways,))],
         2 * tokens * units * width,
         dict(in_specs=[vmem] * 5, out_specs=[vmem, hbm]),
     )

time: 112 us -> 112 us (level)
  transfers between devices with their start and end apart: 2 -> 2, of which waited for: 1 -> 1; matrix products, arithmetic and copies ran while one was open for 0% -> 0% of each run, Pallas kernels for 3% -> 2%
where the time goes in v6:
time: 112 us; the launch traced here: 111 us
  blocking collectives  74.2 us (66%)
  between operations  14.1 us (13%)
  Pallas kernels  7.99 us (7%)
  waiting for transfers between devices  6.23 us (6%)
  local copies, waits for them, and re-layouts  4.85 us (4%)
  starting transfers between devices  3.38 us (3%)
    all_to_all x6, blocking collectives, exchange(): return lax.all_to_all(copies, axis, 0, 0, tiled=True)  74.2 us
    pallas_call x9, Pallas kernels, call(): pl.pallas_call(kernel, out_shape=outs[0] if single else outs, scratch_sha...  7.99 us
    all_to_all x1, waiting for transfers between devices, exchange(): return lax.all_to_all(copies, axis, 0, 0, tiled=True)  5.54 us
    unnamed x12, local copies, waits for them, and re-layouts  4.85 us
    all_to_all x1, starting transfers between devices, exchange(): return lax.all_to_all(copies, axis, 0, 0, tiled=True)  3.34 us
  transfers between devices with their start and end apart: 2, of which 1 were waited for; matrix products, arithmetic and copies ran while one was open for 0% of the time, Pallas kernels for 2%

profile of v6, /device:TPU:1, one launch (start us, length us, event | category | flops | bytes accessed | tf_op | source)
XLA Modules:
  0.0 110.8 jit_solution(14928253664495985279)
XLA Ops:
  7.2 0.0 copy-start.1
  7.2 0.0 all-gather.3.cloned.1.call-start
  7.2 0.7 all-gather.3.cloned.1.call-update
  7.9 0.0 copy-start.2
  7.9 1.0 copy-done.2
  8.9 0.0 copy-start.4
  8.9 0.8 copy-done.4
  9.7 0.3 shard_map.58
  9.9 18.3 %all_to_all.35.parts_ref = f32[8,4,768]{2,1,0:T(4,128)S(1)} all-to-all(f32[8,4,768]{2,1,0:T(4,128)S(1)} %shard_map.58), channel_id=1, replica_groups=mesh['far'=8,'near'=8,'mp'=8] {'mp'}, dimensions={0} | all-to-all | bytes 196608 | tf_op jit(solution)/shard_map/all_to_all | solution.py:194
  28.2 0.0 copy-start
  28.2 1.2 %copy-done = bf16[768,640]{1,0:T(8,128)(2,1)S(1)} copy-done((bf16[768,640]{1,0:T(8,128)(2,1)S(1)}, bf16[768,640]{1,0:T(8,128)(2,1)}, u32[]{:S(2)}) %copy-start) | copy-done | bytes 983064
  29.4 0.0 copy-start.3
  29.4 0.3 shard_map.59
  29.7 11.1 %all_to_all.36.parts_ref = f32[8,4,640]{2,1,0:T(4,128)S(1)} all-to-all(f32[8,4,640]{2,1,0:T(4,128)S(1)} %shard_map.59), channel_id=1, replica_groups=mesh['far'=8,'near'=8,'mp'=8] {'near'}, dimensions={0} | all-to-all | bytes 163840 | tf_op jit(solution)/shard_map/all_to_all | solution.py:194
  40.8 14.1 %all_to_all.37.parts_ref = f32[8,4,640]{2,1,0:T(4,128)S(1)} all-to-all(f32[8,4,640]{2,1,0:T(4,128)S(1)} %shard_map.60), channel_id=1, replica_groups=mesh['far'=8,'near'=8,'mp'=8] {'far'}, dimensions={0} | all-to-all | bytes 163840 | tf_op jit(solution)/shard_map/all_to_all | solution.py:194
  54.9 0.0 copy-done.1
  54.9 0.6 shard_map.61
  55.6 11.2 %all_to_all.38.parts_ref = f32[8,4,896]{2,1,0:T(4,128)S(1)} all-to-all(f32[8,4,896]{2,1,0:T(4,128)S(1)} %get-tuple-element.13), channel_id=1, replica_groups=mesh['far'=8,'near'=8,'mp'=8] {'mp'}, dimensions={0} | all-to-all | bytes 229376 | tf_op jit(solution)/shard_map/all_to_all | solution.py:194
  66.7 0.0 copy-done.3
  66.7 0.2 shard_map.63
  66.9 10.3 %all_to_all.39.parts_ref = f32[8,4,256]{2,1,0:T(4,128)S(1)} all-to-all(f32[8,4,256]{2,1,0:T(4,128)S(1)} %shard_map.63), channel_id=1, replica_groups=mesh['far'=8,'near'=8,'mp'=8] {'near'}, dimensions={0} | all-to-all | bytes 65536 | tf_op jit(solution)/shard_map/all_to_all | solution.py:194
  77.2 9.2 %all_to_all.40.parts_ref = f32[8,4,256]{2,1,0:T(4,128)S(1)} all-to-all(f32[8,4,256]{2,1,0:T(4,128)S(1)} %shard_map.64), channel_id=1, replica_groups=mesh['far'=8,'near'=8,'mp'=8] {'far'}, dimensions={0} | all-to-all | bytes 65536 | tf_op jit(solution)/shard_map/all_to_all | solution.py:194
  86.5 0.0 all-gather.3.cloned.1.call-done
  86.5 0.6 shard_map.65
  87.1 3.3 %all-to-all-start.6 = ((f32[8,4,256]{2,1,0:T(4,128)}), f32[8,4,256]{2,1,0:T(4,128)S(1)}, u32[]{:S(2)}, u32[]{:S(2)}) async-start(f32[8,4,256]{2,1,0:T(4,128)} %shard_map.65), calls=%async_computation.6 | async-start | bytes 65536 | tf_op jit(solution)/shard_map/all_to_all | solution.py:194
  90.5 1.3 %shard_map.62 = (f32[4,640]{1,0:T(4,128)}, f32[32,640]{1,0:T(8,128)S(1)}, f32[16,128]{1,0:T(8,128)S(1)}, bf16[640,768]{1,0:T(8,128)(2,1)S(1)}) custom-call(f32[8,4,896]{2,1,0:T(4,128)S(1)} %all_to_all.38.parts_ref, f32[4,640]{1,0:T(4,128)S(1)} %get-tuple-element.14.raw_ref, bf16[768,640]{1,0:T(8,128)(2,1)S(1)} %copy-done.1), custom_call_target="tpu_custom_call" | custom-call | flops 512000 | bytes 2191360 | tf_op jit(solution)/shard_map/pallas_call | solution.py:183
  91.7 5.5 %all-to-all-done.6.parts_ref = f32[8,4,256]{2,1,0:T(4,128)S(1)} async-done(((f32[8,4,256]{2,1,0:T(4,128)}), f32[8,4,256]{2,1,0:T(4,128)S(1)}, u32[]{:S(2)}, u32[]{:S(2)}) %all-to-all-start.6) | async-done | bytes 32800 | tf_op jit(solution)/shard_map/all_to_all | solution.py:194
  97.2 0.0 copy-start.5
  97.2 1.9 %copy-done.5 = bf16[6144,256]{1,0:T(8,128)(2,1)S(1)} copy-done((bf16[6144,256]{1,0:T(8,128)(2,1)S(1)}, bf16[6144,256]{1,0:T(8,128)(2,1)}, u32[]{:S(2)}) %copy-start.5) | copy-done | bytes 3145752
  99.1 4.8 %shard_map.66 = (f32[4,2048]{1,0:T(4,128)}, bf16[1,640,2048]{2,1,0:T(8,128)(2,1)}) custom-call(f32[8,4,256]{2,1,0:T(4,128)S(1)} %all-to-all-done.6.parts_ref, bf16[640,768]{1,0:T(8,128)(2,1)S(1)} %get-tuple-element.17.turned_ref, bf16[8,768,256]{2,1,0:T(8,128)(2,1)S(1)} %bitcast.1, f32[32,640]{1,0:T(8,128)S(1)} %get-tuple-element.19.wide_ref, ...), custom_call_target="tpu_custom_call" | custom-call | flops 2013265920 | bytes 6905856 | tf_op jit(solution)/shard_map/pallas_call | solution.py:183
  (2 shorter events, 0.0 us)
Async XLA Ops:
  7.2 47.8 %copy-start.1 = (bf16[768,640]{1,0:T(8,128)(2,1)S(1)}, bf16[768,640]{1,0:T(8,128)(2,1)}, u32[]{:S(2)}) copy-start(bf16[768,640]{1,0:T(8,128)(2,1)} %acts_ref.5) | copy-start | bytes 2949124
  7.2 79.3 %all-gather.3.cloned.1.call-start = ((), (), s32[]{:S(2)}) async-start(), calls=%async_computation.7 | async-start | bytes 3538944 | tf_op jit(solution)/shard_map/all_gather | solution.py:206
  7.9 1.0 copy-start.2
  8.9 0.8 copy-start.4
  28.2 1.2 %copy-start = (bf16[768,640]{1,0:T(8,128)(2,1)S(1)}, bf16[768,640]{1,0:T(8,128)(2,1)}, u32[]{:S(2)}) copy-start(bf16[768,640]{1,0:T(8,128)(2,1)} %acts_ref.5) | copy-start | bytes 2949124
  29.4 37.3 %copy-start.3 = (bf16[768,256]{1,0:T(8,128)(2,1)S(1)}, bf16[768,256]{1,0:T(8,128)(2,1)}, u32[]{:S(2)}) copy-start(bf16[768,256]{1,0:T(8,128)(2,1)} %grads_ref.3) | copy-start | bytes 1179652
  87.1 10.1 %all-to-all-start.6 = ((f32[8,4,256]{2,1,0:T(4,128)}), f32[8,4,256]{2,1,0:T(4,128)S(1)}, u32[]{:S(2)}, u32[]{:S(2)}) async-start(f32[8,4,256]{2,1,0:T(4,128)} %shard_map.65), calls=%async_computation.6 | async-start | bytes 65536 | tf_op jit(solution)/shard_map/all_to_all | solution.py:194
  97.2 1.9 %copy-start.5 = (bf16[6144,256]{1,0:T(8,128)(2,1)S(1)}, bf16[6144,256]{1,0:T(8,128)(2,1)}, u32[]{:S(2)}) copy-start(bf16[6144,256]{1,0:T(8,128)(2,1)} %all-gather.3.cloned.1.call-done) | copy-start | bytes 9437188
Sparse Core Ops, SparseCore 0:
  10.1 54.9 all-gather.2
